TPU v7x, 32 devices: a whole 2x2x4 slice. The times are simulated.
32 devices in a mesh: batch: 2 (over core), seq: 16 (over z, y, x).
Axes of the slice: x: 2, y: 2, z: 4, core: 2. Of those that a mesh axis runs over, the one named last changes fastest.
Arguments:
- tokens: bfloat16 [2, 4096, 768], P('batch', 'seq'), may hold values from -6 to 6
- w_query: bfloat16 [768, 768], replicated, may hold values from -0.21875 to 0.21875
- w_key: bfloat16 [768, 768], replicated, may hold values from -0.21875 to 0.21875
- w_value: bfloat16 [768, 768], replicated, may hold values from -0.21875 to 0.21875
- w_out: bfloat16 [768, 768], replicated, may hold values from -0.3125 to 0.3125
- w_up: bfloat16 [768, 3072], replicated, may hold values from -0.21875 to 0.21875
- w_down: bfloat16 [3072, 768], replicated, may hold values from -0.15625 to 0.15625
- gain_mix: float32 [768], replicated, may hold values from 0.5 to 1.5
- gain_ffn: float32 [768], replicated, may hold values from 0.5 to 1.5
- taps: float32 [4, 768], replicated, may hold values from -3 to 3
- rate: float32 [64, 768], replicated, may hold values from 4.8828125e-05 to 0.03125, as said below
- gain_b: float32 [64, 768], replicated, may hold values from -4 to 4
- gain_c: float32 [64, 768], replicated, may hold values from -1 to 1
- skip: float32 [768], replicated, may hold values from -4 to 4
- cotangent: bfloat16 [2, 4096, 768], P('batch', 'seq'), may hold values from -6 to 6
Outputs:
- output: bfloat16 [2, 4096, 768], P('batch', 'seq')
- d_tokens: bfloat16 [2, 4096, 768], P('batch', 'seq')
- d_query: float32 [768, 768], replicated
- d_key: float32 [768, 768], replicated
- d_value: float32 [768, 768], replicated
- d_out: float32 [768, 768], replicated
- d_up: float32 [768, 3072], replicated
- d_down: float32 [3072, 768], replicated
- d_gain_mix: float32 [768], replicated
- d_gain_ffn: float32 [768], replicated
- d_taps: float32 [4, 768], replicated
- d_rate: float32 [64, 768], replicated
- d_gain_b: float32 [64, 768], replicated
- d_gain_c: float32 [64, 768], replicated
- d_skip: float32 [768], replicated
Inputs may be any that keep to these rules, and one draw needn't show every extreme that they name: Every rate is positive.
All inputs are finite; a program needn't handle non-finite values.
Results may differ from a plain program's by a relative error of at most 0.0095.
Values sent between devices are 32-bit elements; how exact they have to be, the bound alone decides.
No kernel may reach another device: no remote copies, remote signals or barrier semaphores. Data moves between devices by JAX's collectives and lax.ppermute only.
A program may use at most 256 MiB of HBM per device.

v0:
```python
import jax
import jax.numpy as jnp
from jax import lax
from jax.sharding import PartitionSpec as P

HIGHEST = lax.Precision.HIGHEST


def passed_along(value, axis, steps):
    count = lax.axis_size(axis)
    leading, last = (max(0, -steps), min(count, count - steps))
    return lax.ppermute(value, axis, [(source, source + steps) for source in range(leading, last)])


def prefix(value, axis, join, neutral, backward):
    count, mine = (lax.axis_size(axis), lax.axis_index(axis))
    pieces = jax.tree.map(lambda part: lax.all_gather(part, axis), value)
    if backward:
        pieces = jax.tree.map(lambda part: part[::-1], pieces)
        mine = count - 1 - mine
    subtotal = jax.tree.map(
        lambda part, zero: jnp.full_like(part, 0) + jnp.asarray(zero, part.dtype), value, neutral
    )

    def lap(position, subtotal):
        longer = join(subtotal, jax.tree.map(lambda part: part[position], pieces))
        return jax.tree.map(lambda new, old: jnp.where(position < mine, new, old), longer, subtotal)

    return lax.fori_loop(0, count - 1, lap, subtotal)


def block_powers(rate, count):
    steps = jnp.arange(count).astype(jnp.float32)
    return jnp.exp(-steps[:, None, None] * rate[None])


def lower_toeplitz(kernel):
    length = kernel.shape[0]
    padded = jnp.concatenate([kernel[:1], jnp.zeros_like(kernel), jnp.flip(kernel[1:], 0)], 0)
    tiled = jnp.tile(padded, (length, 1))[: length * (2 * length - 1)]
    return tiled.reshape(length, 2 * length - 1, kernel.shape[1])[:, :length]


def combine(earlier, later):
    return (earlier[0] * later[0], earlier[1] * later[0] + later[1])


def local_part(inputs, rate, gain_b, gain_c, skip):
    rows, width = inputs.shape
    length = min(16, rows)
    number = rows // length
    scale = gain_b * jnp.sqrt(-jnp.expm1(-2.0 * rate))
    powers = block_powers(rate, length + 1)
    kernel = jnp.einsum("jnc,nc->jc", powers[:length], gain_c * scale, precision=HIGHEST)
    toeplitz = lower_toeplitz(kernel)
    blocks = inputs.reshape(number, length, width)
    inner = jnp.einsum("tsc,isc->itc", toeplitz, blocks, precision=HIGHEST)
    ends = (
        jnp.einsum("snc,isc->inc", jnp.flip(powers[:length], 0), blocks, precision=HIGHEST) * scale
    )
    factor = jnp.broadcast_to(powers[length], ends.shape)
    states = lax.associative_scan(combine, (factor, ends), axis=0)[1]
    return (inner.reshape(rows, width) + skip * inputs, states)


def with_entry(direct, states, entering, rate, gain_c):
    rows, width = direct.shape
    number = states.shape[0]
    length = rows // number
    powers = block_powers(rate, length + 1)
    entry = block_powers(rate * length, number + 1)
    starts = (
        jnp.concatenate([jnp.zeros_like(states[:1]), states[:-1]], 0)
        + entry[:number] * entering[None]
    )
    carried = jnp.einsum("tnc,inc->itc", powers[1:], starts * gain_c, precision=HIGHEST)
    return (direct + carried.reshape(rows, width), states[-1] + entry[number] * entering)


def mixer(inputs, entering, rate, gain_b, gain_c, skip):
    direct, states = local_part(inputs, rate, gain_b, gain_c, skip)
    return with_entry(direct, states, entering, rate, gain_c)


def entry_weights(grad_mixed, rate, gain_c):
    rows, width = grad_mixed.shape
    length = min(16, rows)
    number = rows // length
    powers = block_powers(rate, length + 1)
    entry = block_powers(rate * length, number)
    per_block = jnp.einsum(
        "tnc,itc->inc", powers[1:], grad_mixed.reshape(number, length, width), precision=HIGHEST
    )
    return jnp.sum(per_block * entry, 0) * gain_c


def layer_norm(rows_in, gain):
    centred = rows_in - jnp.mean(rows_in, -1, keepdims=True)
    spread = jnp.mean(centred * centred, -1, keepdims=True)
    return centred * lax.rsqrt(spread + 1e-05) * gain


def shift_mix(key_rows, rim_rows, taps):
    padded = jnp.concatenate([rim_rows, key_rows], 1)
    return (
        taps[0] * padded[:, 3:]
        + taps[1] * padded[:, 2:-1]
        + taps[2] * padded[:, 1:-2]
        + taps[3] * padded[:, :-3]
    )


def gelu_tanh(upper):
    return jax.nn.gelu(upper, approximate=True)


def product(left, right):
    return jnp.dot(left, right, preferred_element_type=jnp.float32)


def weight_grad(left, right):
    return jnp.einsum("ti,tj->ij", left, right, preferred_element_type=jnp.float32)


def back_product(grad_rows, weight):
    return jnp.einsum("tj,ij->ti", grad_rows, weight, preferred_element_type=jnp.float32)


def local(
    tokens,
    w_query,
    w_key,
    w_value,
    w_out,
    w_up,
    w_down,
    gain_mix,
    gain_ffn,
    taps,
    rate,
    gain_b,
    gain_c,
    skip,
    cotangent,
):
    seq_count, rows, width = tokens.shape
    flat_in = tokens.astype(jnp.float32).reshape(seq_count * rows, width)
    normed, norm_pull = jax.vjp(layer_norm, flat_in, gain_mix)
    mixed_in = normed.astype(jnp.bfloat16)
    queries = product(mixed_in, w_query)
    key_rows = product(mixed_in, w_key).reshape(seq_count, rows, width)
    values = product(mixed_in, w_value).reshape(seq_count, rows, width)
    rim_rows = passed_along(key_rows[:, rows - 3 :], "seq", 1)
    shifted, shift_pull = jax.vjp(shift_mix, key_rows, rim_rows, taps)
    inputs = shifted * values
    direct, states = jax.vmap(local_part, in_axes=(0, None, None, None, None))(
        inputs, rate, gain_b, gain_c, skip
    )
    decay_step = jnp.exp(-rate * rows)
    ends = states[:, -1]
    entering = prefix(
        (decay_step, ends), "seq", combine, (jnp.ones_like(decay_step), jnp.zeros_like(ends)), False
    )[1]
    mixed = jax.vmap(with_entry, in_axes=(0, 0, 0, None, None))(
        direct, states, entering, rate, gain_c
    )[0]
    mixed = mixed.reshape(seq_count * rows, width)
    gated = (queries * mixed).astype(jnp.bfloat16)
    hidden = flat_in + product(gated, w_out)
    ffn_normed, ffn_pull = jax.vjp(layer_norm, hidden, gain_ffn)
    ffn_in = ffn_normed.astype(jnp.bfloat16)
    upper = product(ffn_in, w_up)
    activated, gelu_pull = jax.vjp(gelu_tanh, upper)
    act = activated.astype(jnp.bfloat16)
    output = hidden + product(act, w_down)
    grad_out = cotangent.reshape(seq_count * rows, width)
    d_down = weight_grad(act, grad_out)
    grad_act = back_product(grad_out, w_down)
    grad_upper = gelu_pull(grad_act)[0].astype(jnp.bfloat16)
    d_up = weight_grad(ffn_in, grad_upper)
    grad_ffn = back_product(grad_upper, w_up)
    grad_hidden_norm, d_gain_ffn = ffn_pull(grad_ffn)
    grad_hidden = grad_out.astype(jnp.float32) + grad_hidden_norm
    grad_branch = grad_hidden.astype(jnp.bfloat16)
    d_out = weight_grad(gated, grad_branch)
    grad_gated = back_product(grad_branch, w_out)
    grad_queries = (grad_gated * mixed).astype(jnp.bfloat16)
    grad_mixed = (grad_gated * queries).reshape(seq_count, rows, width)
    towards = jax.vmap(entry_weights, in_axes=(0, None, None))(grad_mixed, rate, gain_c)
    adjoint = prefix(
        (decay_step, towards),
        "seq",
        combine,
        (jnp.ones_like(decay_step), jnp.zeros_like(towards)),
        True,
    )[1]

    def mixer_back(inputs_one, entering_one, grad_one, adjoint_one):
        pullback = jax.vjp(mixer, inputs_one, entering_one, rate, gain_b, gain_c, skip)[1]
        return pullback((grad_one, adjoint_one))

    grad_inputs, _, d_rate, d_gain_b, d_gain_c, d_skip = jax.vmap(mixer_back)(
        inputs, entering, grad_mixed, adjoint
    )
    d_rate = jnp.sum(d_rate, 0)
    d_gain_b = jnp.sum(d_gain_b, 0)
    d_gain_c = jnp.sum(d_gain_c, 0)
    d_skip = jnp.sum(d_skip, 0)
    grad_values = (grad_inputs * shifted).astype(jnp.bfloat16).reshape(seq_count * rows, width)
    grad_shifted = grad_inputs * values
    grad_keys_local, grad_rim, d_taps = shift_pull(grad_shifted)
    rim_back = passed_along(grad_rim, "seq", -1)
    grad_keys = jnp.concatenate(
        [grad_keys_local[:, : rows - 3], grad_keys_local[:, rows - 3 :] + rim_back], 1
    )
    grad_keys = grad_keys.astype(jnp.bfloat16).reshape(seq_count * rows, width)
    d_query = weight_grad(mixed_in, grad_queries)
    d_key = weight_grad(mixed_in, grad_keys)
    d_value = weight_grad(mixed_in, grad_values)
    grad_normed = (
        back_product(grad_queries, w_query)
        + back_product(grad_keys, w_key)
        + back_product(grad_values, w_value)
    )
    grad_input_norm, d_gain_mix = norm_pull(grad_normed)
    d_tokens = (grad_hidden + grad_input_norm).astype(jnp.bfloat16).reshape(seq_count, rows, width)
    small_parts = jnp.concatenate(
        [
            d_gain_mix,
            d_gain_ffn,
            d_taps.reshape(-1),
            d_rate.reshape(-1),
            d_gain_b.reshape(-1),
            d_gain_c.reshape(-1),
            d_skip,
        ]
    )
    flat_grads = (
        d_query.reshape(-1),
        d_key.reshape(-1),
        d_value.reshape(-1),
        d_out.reshape(-1),
        d_up.reshape(-1),
        d_down.reshape(-1),
        small_parts,
    )
    partial_all = (
        lax.psum_scatter(flat_grads[0], ("batch", "seq"), scatter_dimension=0, tiled=True),
        lax.psum_scatter(flat_grads[1], ("batch", "seq"), scatter_dimension=0, tiled=True),
        lax.psum_scatter(flat_grads[2], ("batch", "seq"), scatter_dimension=0, tiled=True),
        lax.psum_scatter(flat_grads[3], ("batch", "seq"), scatter_dimension=0, tiled=True),
        lax.psum_scatter(flat_grads[4], ("batch", "seq"), scatter_dimension=0, tiled=True),
        lax.psum_scatter(flat_grads[5], ("batch", "seq"), scatter_dimension=0, tiled=True),
        lax.psum_scatter(flat_grads[6], ("batch", "seq"), scatter_dimension=0, tiled=True),
    )
    summed = (
        lax.all_gather(partial_all[0], ("batch", "seq"), axis=0, tiled=True),
        lax.all_gather(partial_all[1], ("batch", "seq"), axis=0, tiled=True),
        lax.all_gather(partial_all[2], ("batch", "seq"), axis=0, tiled=True),
        lax.all_gather(partial_all[3], ("batch", "seq"), axis=0, tiled=True),
        lax.all_gather(partial_all[4], ("batch", "seq"), axis=0, tiled=True),
        lax.all_gather(partial_all[5], ("batch", "seq"), axis=0, tiled=True),
        lax.all_gather(partial_all[6], ("batch", "seq"), axis=0, tiled=True),
    )
    state_size = rate.shape[0]
    small_sum = summed[6]
    offsets = [
        0,
        width,
        2 * width,
        6 * width,
        6 * width + state_size * width,
        6 * width + 2 * state_size * width,
        6 * width + 3 * state_size * width,
        7 * width + 3 * state_size * width,
    ]
    pieces = [small_sum[offsets[i] : offsets[i + 1]] for i in range(7)]
    return (
        output.astype(jnp.bfloat16).reshape(seq_count, rows, width),
        d_tokens,
        summed[0].reshape(width, width),
        summed[1].reshape(width, width),
        summed[2].reshape(width, width),
        summed[3].reshape(width, width),
        summed[4].reshape(w_up.shape),
        summed[5].reshape(w_down.shape),
        pieces[0],
        pieces[1],
        pieces[2].reshape(taps.shape),
        pieces[3].reshape(rate.shape),
        pieces[4].reshape(rate.shape),
        pieces[5].reshape(rate.shape),
        pieces[6],
    )


def solution(mesh):
    in_specs = (
        P("batch", "seq", None),
        P(),
        P(),
        P(),
        P(),
        P(),
        P(),
        P(),
        P(),
        P(),
        P(),
        P(),
        P(),
        P(),
        P("batch", "seq", None),
    )
    out_specs = (
        P("batch", "seq", None),
        P("batch", "seq", None),
        P(),
        P(),
        P(),
        P(),
        P(),
        P(),
        P(),
        P(),
        P(),
        P(),
        P(),
        P(),
        P(),
    )
    return jax.shard_map(local, mesh=mesh, in_specs=in_specs, out_specs=out_specs, check_vma=False)
```

profile of v0, /device:TPU:0, one launch (start us, length us, event | category | flops | bytes accessed | tf_op | source)
XLA Modules:
  0.0 1667.2 jit_solution(5704178981747944809)
XLA Ops:
  14.1 5.4 collective-permute-start
  31.1 6.9 copy.220
  41.4 4.9 copy.217
  46.4 11.2 fusion.116
  57.5 6.6 copy.221
  80.8 4.4 pad.215
  87.9 7.0 pad.448
  102.7 6.8 copy.226
  120.0 5.9 copy.284
  126.4 7.1 pad.218
  136.9 7.3 pad.217
  144.1 14.8 convolution_bitcast_fusion.2
  158.9 5.9 copy.218
  164.8 4.7 slice_add_fusion
  169.5 18.1 %while.28 = (s32[]{:T(128)}, f32[1,64,768]{2,1,0:T(8,128)S(1)}, s32[]{:T(128)}, f32[16,64,768]{2,1,0:T(8,128)}, f32[16,1,64,768]{3,2,1,0:T(8,128)}, /*index=5*/s32[]{:T(128)}, s32[]{:T(128)}) while((s32[]{:T(128)}, f32[1,64,768]{2,1,0:T(8,128)S(1)}, s32[]{:T(128)}, f32[16,64,768]{2,1,0:T(8,128)}, f32[16,1,64,768]{3,2,1,0:T(8,128)}, ...), condition=%wide.region_3.4_spmd.clone, body=%wide.region_2.3_spmd.clone.sunk | while | flops 196612 | bytes 786533 | solution.py:29
  191.8 6.8 copy.225
  198.7 15.2 convolution_bitcast_fusion.1
  213.9 5.9 copy.227
  224.1 4.6 fusion.90
  238.1 6.0 copy.228
  244.1 13.9 fusion.2
  261.6 6.3 copy.246
  271.8 5.9 copy.266
  277.8 14.0 fusion.118
  291.7 6.6 copy.235
  298.3 6.3 broadcast_multiply_fusion
  306.4 6.0 copy.232
  312.4 9.0 fusion.17
  324.5 6.4 reshape.545
  343.3 11.1 fusion.3
  354.5 6.5 copy.243
  361.9 4.7 multiply_reduce_fusion.3
  373.5 5.9 copy.288
  384.8 7.9 fusion.63
  392.7 10.7 reshape.527
  417.5 18.0 %while.29 = (s32[]{:T(128)}, f32[1,64,768]{2,1,0:T(8,128)S(1)}, s32[]{:T(128)}, f32[16,64,768]{2,1,0:T(8,128)}, f32[16,1,64,768]{3,2,1,0:T(8,128)}, /*index=5*/s32[]{:T(128)}, s32[]{:T(128)}) while((s32[]{:T(128)}, f32[1,64,768]{2,1,0:T(8,128)S(1)}, s32[]{:T(128)}, f32[16,64,768]{2,1,0:T(8,128)}, f32[16,1,64,768]{3,2,1,0:T(8,128)}, ...), condition=%wide.region_10.11_spmd.clone, body=%wide.region_9.10_spmd.clone.sunk | while | flops 196612 | bytes 786533 | solution.py:29
  465.5 4.5 pad.242
  470.0 4.4 pad.243
  485.9 6.7 multiply_add_fusion
  494.0 4.5 pad.244
  499.1 7.0 pad.245
  506.2 4.5 pad.223
  510.7 6.4 fusion.15
  519.0 7.0 copy.236
  526.0 12.9 fusion.119
  538.8 13.6 add_bitcast_fusion
  552.4 5.2 copy.239
  563.7 7.1 pad.265
  570.8 7.0 pad.266
  577.8 6.5 pad.257
  584.3 10.9 fusion.121
  595.3 6.5 copy.247
  605.8 4.5 add_reduce_fusion
  663.2 119.1 %all-reduce.67.cloned.1.call-done = f32[152832]{0:T(1024)} async-done(((f32[152832]{0:T(1024)}), f32[152832]{0:T(1024)}) %all-reduce.67.cloned.1.call-update) | async-done | bytes 611344
  784.2 455.6 %all-reduce.69.cloned.1.call-done = (f32[589824]{0:T(1024)}, f32[589824]{0:T(1024)}, f32[589824]{0:T(1024)}, f32[589824]{0:T(1024)}, f32[2359296]{0:T(1024)}, /*index=5*/f32[2359296]{0:T(1024)}, f32[152832]{0:T(1024)}) async-done(((f32[589824]{0:T(1024)}, f32[589824]{0:T(1024)}, f32[589824]{0:T(1024)}, f32[589824]{0:T(1024)}, f32[2359296]{0:T(1024)}, /*index=5*/f32[2359296]{0:T(1024)}, f32[152832]{0:T(1024)}), ...) | async-done | bytes 28922896
  1250.1 6.2 fusion.21
  1261.6 38.4 %all-gather.16.cloned.1.call-done = f32[589824]{0:T(1024)} async-done(((f32[18432]{0:T(1024)}), f32[589824]{0:T(1024)}) %all-gather.16.cloned.1.call-update) | async-done | bytes 2359312 | tf_op jit(solution)/shard_map/all_gather | solution.py:258
  1303.4 56.7 %all-gather.18.cloned.1.call-done = f32[589824]{0:T(1024)} async-done(((f32[18432]{0:T(1024)}), f32[589824]{0:T(1024)}) %all-gather.18.cloned.1.call-update) | async-done | bytes 2359312 | tf_op jit(solution)/shard_map/all_gather | solution.py:259
  1363.4 56.7 %all-gather.20.cloned.1.call-done = f32[589824]{0:T(1024)} async-done(((f32[18432]{0:T(1024)}), f32[589824]{0:T(1024)}) %all-gather.20.cloned.1.call-update) | async-done | bytes 2359312 | tf_op jit(solution)/shard_map/all_gather | solution.py:260
  1423.5 56.7 %all-gather.14.cloned.1.call-done = f32[589824]{0:T(1024)} async-done(((f32[18432]{0:T(1024)}), f32[589824]{0:T(1024)}) %all-gather.14.cloned.1.call-update) | async-done | bytes 2359312 | tf_op jit(solution)/shard_map/all_gather | solution.py:257
  1483.5 81.3 %all-gather.22.cloned.1.call-done = f32[2359296]{0:T(1024)} async-done(((f32[73728]{0:T(1024)}), f32[2359296]{0:T(1024)}) %all-gather.22.cloned.1.call-update) | async-done | bytes 9437200 | tf_op jit(solution)/shard_map/all_gather | solution.py:261
  1564.9 10.9 reshape.526
  1575.8 73.1 %all-gather.24.cloned.1.call-done = f32[2359296]{0:T(1024)} async-done(((f32[73728]{0:T(1024)}), f32[2359296]{0:T(1024)}) %all-gather.24.cloned.1.call-update) | async-done | bytes 9437200 | tf_op jit(solution)/shard_map/all_gather | solution.py:262
  1648.9 11.3 reshape.528
  (495 shorter events, 306.6 us)
Async XLA Ops:
  7.2 31.6 %copy-start = (bf16[768,768]{1,0:T(8,128)(2,1)S(1)}, bf16[768,768]{1,0:T(8,128)(2,1)}, u32[]{:S(2)}) copy-start(bf16[768,768]{1,0:T(8,128)(2,1)} %param.22) | copy-start | bytes 3538948
  7.2 12.4 copy-start.69
  7.2 12.5 copy-start.90
  7.2 12.7 copy-start.71
  7.2 162.3 %all-gather.26.cloned.1.call-start = ((), (), s32[]{:S(2)}) async-start(), calls=%async_computation.7 | async-start | bytes 3342336 | tf_op jit(solution)/shard_map/all_gather | solution.py:17
  9.1 160.5 %all-gather.12.cloned.1.call-start = ((), (), s32[]{:S(2)}) async-start(), calls=%async_computation | async-start | bytes 3342336 | tf_op jit(solution)/shard_map/all_gather | solution.py:17
  11.5 9.3 copy-start.110
  13.5 25.4 %copy-start.24 = (f32[256,768]{1,0:T(8,128)}, f32[256,768]{1,0:T(8,128)S(1)}, u32[]{:S(2)}) copy-start(f32[256,768]{1,0:T(8,128)S(1)} %fusion.96) | copy-start | bytes 2359300
  14.1 24.7 %collective-permute-start = (f32[1,3,768]{2,1,0:T(4,128)}, f32[1,3,768]{2,1,0:T(4,128)}, u32[]{:S(2)}, u32[]{:S(2)}) collective-permute-start(f32[1,3,768]{2,1,0:T(4,128)} %slice.314), channel_id=1, source_target_pairs={{0,1},{1,2},{2,3},{3,4},{4,5},{5,6},{6,7},{7,8},{8,9},{9,10},{10,1... | collective-permute-start | bytes 27656 | tf_op jit(solution)/shard_map/ppermute | solution.py:12
  20.9 45.5 %copy-start.27 = (f32[64,768]{1,0:T(8,128)}, f32[64,768]{1,0:T(8,128)S(1)}, u32[]{:S(2)}) copy-start(f32[64,768]{1,0:T(8,128)S(1)} %slice_bitcast_fusion) | copy-start | bytes 589828
  21.6 56.6 %copy-start.30 = (f32[64,768]{1,0:T(8,128)}, f32[64,768]{1,0:T(8,128)S(1)}, u32[]{:S(2)}) copy-start(f32[64,768]{1,0:T(8,128)S(1)} %get-tuple-element.334) | copy-start | bytes 589828
  27.2 11.6 copy-start.96
  31.1 6.9 copy-start.47
  31.1 7.7 copy-start.2
  31.1 7.8 copy-start.89
  57.5 6.6 copy-start.78
  96.5 317.1 %all-gather.28.cloned.1.call-start = ((), (), s32[]{:S(2)}) async-start(), calls=%async_computation.8 | async-start | bytes 3342336 | tf_op jit(solution)/shard_map/all_gather | solution.py:17
  97.9 11.6 copy-start.80
  169.5 18.2 %copy-start.72 = (f32[64,768]{1,0:T(8,128)S(1)}, f32[64,768]{1,0:T(8,128)}, u32[]{:S(2)}) copy-start(f32[64,768]{1,0:T(8,128)} %param.31) | copy-start | bytes 589828
  169.5 18.2 %copy-start.113 = (f32[17]{0:T(128)S(1)}, f32[17]{0:T(128)}, u32[]{:S(2)}) copy-start(f32[17]{0:T(128)} %copy-done.112) | copy-start | bytes 208
  223.8 10.5 copy-start.16
  223.8 10.5 copy-start.95
  224.1 10.2 copy-start.104
  224.1 7.9 slice-start.6
  261.5 520.7 %all-reduce.67.cloned.1.call-start = ((), (), s32[]{:S(2)}) async-start(), calls=%async_computation.9 | async-start | bytes 1228800
  450.1 10.2 copy-start.8
  452.6 7.8 copy-start.82
  452.6 7.8 copy-start.83
  464.5 9.8 copy-start.60
  470.0 7.0 copy-start.59
  476.9 6.5 copy-start.77
  476.9 9.0 copy-start.29
  476.9 9.0 slice-start.5
  498.4 7.8 copy-start.39
  510.7 6.4 copy-start.79
  519.0 19.8 %slice-start = ((s8[6291456]{0:T(1024)(128)(4,1)}), s8[2097152]{0:T(1024)(128)(4,1)S(1)}, s32[]{:S(2)}) async-start(s8[6291456]{0:T(1024)(128)(4,1)} %bitcast.346), calls=%async_computation.11 | async-start | bytes 4194304
  526.0 12.9 slice-start.1
  601.8 8.5 copy-start.73
  601.8 8.5 copy-start.87
  605.8 6.5 copy-start.11
  605.8 6.5 copy-start.70
  605.8 6.5 copy-start.114
  612.3 13.7 copy-start.101
  616.5 12.7 copy-start.43
  616.5 12.7 copy-start.45
  627.8 10.8 collective-permute-start.1
  632.4 7.1 copy-start.48
  640.7 7.3 copy-start.85
  640.7 8.9 copy-start.86
  640.7 10.5 copy-start.102
  640.7 11.9 copy-start.50
  641.4 9.8 copy-start.106
  652.5 587.3 %all-reduce.69.cloned.1.call-start = ((), (), s32[]{:S(2)}) async-start(), calls=%async_computation.10 | async-start | bytes 57851904
  784.1 465.9 %copy-start.17 = (f32[256,768]{1,0:T(8,128)S(1)}, f32[256,768]{1,0:T(8,128)}, u32[]{:S(2)}) copy-start(f32[256,768]{1,0:T(8,128)} %copy-done.16) | copy-start | bytes 2359300
  784.1 515.9 %all-gather.16.cloned.1.call-start = ((), (), s32[]{:S(2)}) async-start(), calls=%async_computation.2 | async-start | bytes 2433024 | tf_op jit(solution)/shard_map/all_gather | solution.py:258
  1241.3 118.7 %all-gather.18.cloned.1.call-start = ((), (), s32[]{:S(2)}) async-start(), calls=%async_computation.3 | async-start | bytes 2433024 | tf_op jit(solution)/shard_map/all_gather | solution.py:259
  1242.9 177.2 %all-gather.20.cloned.1.call-start = ((), (), s32[]{:S(2)}) async-start(), calls=%async_computation.4 | async-start | bytes 2433024 | tf_op jit(solution)/shard_map/all_gather | solution.py:260
  1244.5 235.6 %all-gather.14.cloned.1.call-start = ((), (), s32[]{:S(2)}) async-start(), calls=%async_computation.1 | async-start | bytes 2433024 | tf_op jit(solution)/shard_map/all_gather | solution.py:257
  1246.1 318.7 %all-gather.22.cloned.1.call-start = ((), (), s32[]{:S(2)}) async-start(), calls=%async_computation.5 | async-start | bytes 9732096 | tf_op jit(solution)/shard_map/all_gather | solution.py:261
  1247.9 401.0 %all-gather.24.cloned.1.call-start = ((), (), s32[]{:S(2)}) async-start(), calls=%async_computation.6 | async-start | bytes 9732096 | tf_op jit(solution)/shard_map/all_gather | solution.py:262
  1250.0 6.2 copy-start.115
  1250.0 6.2 copy-start.34
  1250.0 6.2 copy-start.56
  1250.1 7.3 copy-start.88
  (77 other events, 232.8 us)
Sparse Core Ops, SparseCore 0:
  10.8 70.8 all-gather.25
  96.6 67.8 all-gather.11
  261.6 67.7 all-gather.27
  652.6 129.5 all-reduce.66
  790.2 449.5 all-reduce.68
  1243.5 56.4 all-gather.15
  1303.9 56.1 all-gather.17
  1363.9 56.1 all-gather.19
  1424.0 56.1 all-gather.13
  1483.9 80.9 all-gather.21
  1568.2 80.6 all-gather.23
where the time goes:
time: 1680 us; the launch traced here: 1670 us
  waiting for transfers between devices  938 us (56%)
  local copies, waits for them, and re-layouts  386 us (23%)
  matrix products  177 us (11%)
  other arithmetic  143 us (9%)
    unnamed x13, waiting for transfers between devices  575 us
    pad x24, local copies, waits for them, and re-layouts, local_part(): states = lax.associative_scan(combine, (factor, ends), axis=0)[1]  89.8 us
    all_gather x1, waiting for transfers between devices, local(): lax.all_gather(partial_all[4], ('batch', 'seq'), axis=0, tiled=True)  81.3 us
    all_gather x1, waiting for transfers between devices, local(): lax.all_gather(partial_all[5], ('batch', 'seq'), axis=0, tiled=True)  73.1 us
    unnamed x275, local copies, waits for them, and re-layouts  64.5 us
    all_gather x1, waiting for transfers between devices, local(): lax.all_gather(partial_all[0], ('batch', 'seq'), axis=0, tiled=True)  56.7 us
    all_gather x1, waiting for transfers between devices, local(): lax.all_gather(partial_all[2], ('batch', 'seq'), axis=0, tiled=True)  56.7 us
    all_gather x1, waiting for transfers between devices, local(): lax.all_gather(partial_all[3], ('batch', 'seq'), axis=0, tiled=True)  56.7 us
  transfers between devices with their start and end apart: 13, of which 8 were waited for; matrix products, arithmetic and copies ran while one was open for 22% of the time, Pallas kernels for 0%

commit v1 on v0

v1 whole, which is shorter than its diff:
```python
import jax
import jax.numpy as jnp
from jax import lax
from jax.experimental import pallas as pl
from jax.experimental.pallas import tpu as pltpu
from jax.sharding import PartitionSpec as P

F32 = jnp.float32
BF16 = jnp.bfloat16
LANES = 128


def cost(flops, moved):
    return pl.CostEstimate(flops=flops, bytes_accessed=moved, transcendentals=0)


def col_spec(rows):
    return pl.BlockSpec((rows, LANES), lambda g: (0, g))


def per_group(kernel, ins, outs, scratch, flops):
    width = ins[0].shape[1]
    moved = sum(x.size * x.dtype.itemsize for x in ins) + sum(
        rows * width * jnp.dtype(kind).itemsize for rows, kind in outs
    )
    return pl.pallas_call(
        kernel,
        grid=(width // LANES,),
        in_specs=[col_spec(x.shape[0]) for x in ins],
        out_specs=[col_spec(rows) for rows, _ in outs],
        out_shape=[jax.ShapeDtypeStruct((rows, width), kind) for rows, kind in outs],
        scratch_shapes=scratch,
        cost_estimate=cost(flops, moved),
        compiler_params=pltpu.CompilerParams(vmem_limit_bytes=32 * 1024 * 1024),
    )(*ins)


def folded(product):
    return jnp.sum(product.reshape(product.shape[0] // 8, 8, product.shape[1]), 0)


def unfold(parts_ref, rows):
    total = parts_ref[pl.ds(0, rows, stride=8), :]
    for s in range(1, 8):
        total = total + parts_ref[pl.ds(s, rows, stride=8), :]
    return total


def ends_kernel(key_ref, value_ref, rim_ref, taps_ref, rate_ref, shifted_ref, inputs_ref, end_ref, pad):
    rows = key_ref.shape[0]
    pad[0:8, :] = rim_ref[...]
    pad[8:, :] = key_ref[...]
    shifted = taps_ref[0:1, :] * pad[8:, :]
    for j in range(1, 4):
        shifted = shifted + taps_ref[j : j + 1, :] * pad[8 - j : 8 - j + rows, :]
    shifted_ref[...] = shifted
    inputs_ref[...] = shifted * value_ref[...]
    decay = jnp.exp(-rate_ref[...])

    def lap(i, state):
        for k in range(16):
            state = decay * state + inputs_ref[pl.ds(i * 16 + k, 1), :]
        return state

    end_ref[...] = lax.fori_loop(0, rows // 16, lap, jnp.zeros_like(decay))


def mix_kernel(
    inputs_ref, query_ref, enter_ref, rate_ref, read_ref, skip_ref, mixed_ref, gated_ref, parts
):
    rows = inputs_ref.shape[0]
    decay = jnp.exp(-rate_ref[...])
    read = read_ref[...]

    def lap(i, state):
        for k in range(16):
            t = i * 16 + k
            state = decay * state + inputs_ref[pl.ds(t, 1), :]
            parts[pl.ds(pl.multiple_of(t * 8, 8), 8), :] = folded(read * state)
        return state

    lax.fori_loop(0, rows // 16, lap, enter_ref[...])
    mixed = unfold(parts, rows) + skip_ref[...] * inputs_ref[...]
    mixed_ref[...] = mixed
    gated_ref[...] = (query_ref[...] * mixed).astype(BF16)


def towards_kernel(
    grad_ref, query_ref, mixed_ref, rate_ref, grad_query_ref, grad_mixed_ref, start_ref
):
    rows = grad_ref.shape[0]
    grad_query_ref[...] = (grad_ref[...] * mixed_ref[...]).astype(BF16)
    grad_mixed_ref[...] = grad_ref[...] * query_ref[...]
    decay = jnp.exp(-rate_ref[...])

    def lap(i, state):
        for k in range(16):
            state = decay * state + grad_mixed_ref[pl.ds(rows - 1 - i * 16 - k, 1), :]
        return state

    start_ref[...] = lax.fori_loop(0, rows // 16, lap, jnp.zeros_like(decay))


def back_kernel(
    grad_ref,
    inputs_ref,
    shifted_ref,
    value_ref,
    key_ref,
    rim_ref,
    taps_ref,
    rate_ref,
    read_ref,
    skip_ref,
    enter_ref,
    adjoint_ref,
    grad_value_ref,
    grad_key_ref,
    head_ref,
    sum_ref,
    slope_ref,
    small_ref,
    parts,
    pad,
):
    rows = grad_ref.shape[0]
    decay = jnp.exp(-rate_ref[...])
    read = read_ref[...]
    zero = jnp.zeros_like(decay)

    def lap(i, carry):
        adjoint, ramp, total, slope = carry
        for k in range(8):
            t = rows - 1 - i * 8 - k
            entry = inputs_ref[pl.ds(t, 1), :]
            slope = slope + entry * ramp
            adjoint = decay * adjoint + grad_ref[pl.ds(t, 1), :]
            total = total + entry * adjoint
            parts[pl.ds(pl.multiple_of(t * 8, 8), 8), :] = folded(read * adjoint)
            ramp = decay * ramp + adjoint
        return adjoint, ramp, total, slope

    _, ramp, total, slope = lax.fori_loop(
        0, rows // 8, lap, (adjoint_ref[...], zero, zero, zero)
    )
    sum_ref[...] = total
    slope_ref[...] = slope + enter_ref[...] * ramp
    grad = grad_ref[...]
    grad_inputs = unfold(parts, rows) + skip_ref[...] * grad
    grad_value_ref[...] = (grad_inputs * shifted_ref[...]).astype(BF16)
    grad_shifted = grad_inputs * value_ref[...]
    pad[0:rows, :] = grad_shifted
    pad[rows:, :] = jnp.zeros_like(head_ref)
    head_ref[...] = pad[0:8, :]
    grad_key = taps_ref[0:1, :] * grad_shifted
    for j in range(1, 4):
        grad_key = grad_key + taps_ref[j : j + 1, :] * pad[j : j + rows, :]
    grad_key_ref[...] = grad_key
    pad[0:8, :] = rim_ref[...]
    pad[8:, :] = key_ref[...]
    small = [
        jnp.sum(grad_shifted * pad[8 - j : 8 - j + rows, :], 0, keepdims=True) for j in range(4)
    ]
    small.append(jnp.sum(grad * inputs_ref[...], 0, keepdims=True))
    small.append(jnp.zeros((3, LANES), F32))
    small_ref[...] = jnp.concatenate(small, 0)


def bits_of(count):
    out, step = [], 1
    while step < count:
        out.append(step)
        step *= 2
    return out


class Wires:
    def __init__(self):
        self.batch, self.seq = lax.axis_size("batch"), lax.axis_size("seq")
        bits = bits_of(self.seq)
        self.orders = (tuple(bits), tuple(bits[1::-1] + bits[2:]))
        self.spare = bits_of(self.batch)[1:]
        self.core = lax.axis_index("batch") % 2
        self.place = lax.axis_index("seq")
        self.steps = len(bits)

    def bit(self, step, core=None):
        core = self.core if core is None else core
        first, second = ((self.place // order[step]) % 2 for order in self.orders)
        return jnp.where(core == 0, first, second)

    def swap(self, value, step):
        pairs = [
            (b * self.seq + s, b * self.seq + (s ^ self.orders[b % 2][step]))
            for b in range(self.batch)
            for s in range(self.seq)
        ]
        return lax.ppermute(value, ("batch", "seq"), pairs)

    def swap_batch(self, value, step):
        return lax.ppermute(value, "batch", [(b, b ^ step) for b in range(self.batch)])

    def scatter_sum(self, send, keep):
        keep_in, received = keep, self.swap_batch(send, 1)
        for step in range(self.steps):
            mine = self.bit(step)
            send = half(keep_in, 1 - mine) + half(received, 1 - mine)
            arriving = self.swap(send, step)
            keep_in = half(keep_in, mine) + half(received, mine)
            received = arriving
        total = keep_in + received
        for step in self.spare:
            total = total + self.swap_batch(total, step)
        return total

    def gather(self, block):
        for step in range(self.steps - 1, 0, -1):
            mine = self.bit(step) == 0
            arriving = self.swap(block, step)
            block = jnp.concatenate(
                [jnp.where(mine, block, arriving), jnp.where(mine, arriving, block)], 0
            )
        other = self.swap(block, 0)
        return block, other, self.swap_batch(block, 1), self.swap_batch(other, 1)

    def halves(self, quarters):
        own, other, far, far_other = quarters
        mine = self.bit(0) == 0
        theirs = self.bit(0, 1 - self.core) == 0
        first = self.core == 0
        here = (jnp.where(mine, own, other), jnp.where(mine, other, own))
        there = (jnp.where(theirs, far, far_other), jnp.where(theirs, far_other, far))
        return [
            jnp.concatenate([jnp.where(first, h, t) for h, t in zip(here, there)], 0),
            jnp.concatenate([jnp.where(first, t, h) for h, t in zip(here, there)], 0),
        ]


def half(value, which):
    rows = value.shape[0] // 2
    return lax.dynamic_slice_in_dim(value, which * rows, rows, 0)


def prefix(ends, rate, rows, backward):
    count = lax.axis_size("seq")
    place = lax.axis_index("seq")
    rank = count - 1 - place if backward else place
    total = ends
    entering = jnp.zeros_like(ends)
    steps = bits_of(count)
    for step in steps:
        arriving = lax.ppermute(total, "seq", [(s, s ^ step) for s in range(count)])
        upper = (rank // step) % 2 == 1
        behind = ((rank % step) * rows).astype(F32)
        entering = jnp.where(upper, entering + jnp.exp(-rate * behind) * arriving, entering)
        if step != steps[-1]:
            early = jnp.where(upper, arriving, total)
            late = jnp.where(upper, total, arriving)
            total = jnp.exp(-rate * (step * rows)) * early + late
    return entering


def layer_norm(rows_in, gain):
    centred = rows_in - jnp.mean(rows_in, -1, keepdims=True)
    spread = jnp.mean(centred * centred, -1, keepdims=True)
    return centred * lax.rsqrt(spread + 1e-05) * gain


def gelu_tanh(upper):
    return jax.nn.gelu(upper, approximate=True)


def product(left, right):
    return jnp.dot(left, right, preferred_element_type=F32)


def weight_grad(left, right):
    return jnp.einsum("ti,tj->ij", left, right, preferred_element_type=F32)


def back_product(grad_rows, weight):
    return jnp.einsum("tj,ij->ti", grad_rows, weight, preferred_element_type=F32)


def local(
    tokens,
    w_query,
    w_key,
    w_value,
    w_out,
    w_up,
    w_down,
    gain_mix,
    gain_ffn,
    taps,
    rate,
    gain_b,
    gain_c,
    skip,
    cotangent,
):
    _, rows, width = tokens.shape
    count = lax.axis_size("seq")
    states = rate.shape[0]
    wires = Wires()
    skip_row = skip.reshape(1, width)
    scale = gain_b * jnp.sqrt(-jnp.expm1(-2.0 * rate))
    read = gain_c * scale

    flat_in = tokens.astype(F32).reshape(rows, width)
    normed, norm_pull = jax.vjp(layer_norm, flat_in, gain_mix)
    mixed_in = normed.astype(BF16)
    rim_own = product(layer_norm(flat_in[rows - 8 :], gain_mix).astype(BF16), w_key)
    rim = lax.ppermute(rim_own, "seq", [(s, s + 1) for s in range(count - 1)])
    queries = product(mixed_in, w_query)
    key_rows = product(mixed_in, w_key)
    values = product(mixed_in, w_value)
    element = rows * states * width
    shifted, inputs, ends = per_group(
        ends_kernel,
        (key_rows, values, rim, taps, rate),
        ((rows, F32), (rows, F32), (states, F32)),
        [pltpu.VMEM((rows + 8, LANES), F32)],
        2 * element,
    )
    entering = prefix(ends, rate, rows, False)
    mixed, gated = per_group(
        mix_kernel,
        (inputs, queries, entering, rate, read, skip_row),
        ((rows, F32), (rows, BF16)),
        [pltpu.VMEM((rows * 8, LANES), F32)],
        4 * element,
    )
    hidden = flat_in + product(gated, w_out)
    ffn_normed, ffn_pull = jax.vjp(layer_norm, hidden, gain_ffn)
    ffn_in = ffn_normed.astype(BF16)
    upper = product(ffn_in, w_up)
    activated, gelu_pull = jax.vjp(gelu_tanh, upper)
    act = activated.astype(BF16)
    grad_out = cotangent.reshape(rows, width)

    def by_columns(left, right):
        return (
            weight_grad(half_columns(left, 1 - wires.core), right),
            weight_grad(half_columns(left, wires.core), right),
        )

    def by_tensor(first, second):
        picked = [jnp.where(wires.core == 0, a, b) for a, b in zip(first, second)]
        others = [jnp.where(wires.core == 0, b, a) for a, b in zip(first, second)]
        return weight_grad(*others), weight_grad(*picked)

    middle = act.shape[1] // 2
    chunks = []
    chunks.append(wires.scatter_sum(*by_columns(act[:, :middle], grad_out)))
    chunks.append(wires.scatter_sum(*by_columns(act[:, middle:], grad_out)))
    grad_act = back_product(grad_out, w_down)
    grad_upper = gelu_pull(grad_act)[0].astype(BF16)
    chunks.append(wires.scatter_sum(*by_columns(ffn_in[:, : width // 2], grad_upper)))
    chunks.append(wires.scatter_sum(*by_columns(ffn_in[:, width // 2 :], grad_upper)))
    output = hidden + product(act, w_down)
    grad_ffn = back_product(grad_upper, w_up)
    grad_hidden_norm, d_gain_ffn = ffn_pull(grad_ffn)
    grad_hidden = grad_out.astype(F32) + grad_hidden_norm
    grad_branch = grad_hidden.astype(BF16)
    grad_gated = back_product(grad_branch, w_out)
    grad_queries, grad_mixed, starts = per_group(
        towards_kernel,
        (grad_gated, queries, mixed, rate),
        ((rows, BF16), (rows, F32), (states, F32)),
        [],
        2 * element,
    )
    chunks.append(wires.scatter_sum(*by_tensor((gated, grad_branch), (mixed_in, grad_queries))))
    adjoint = prefix(starts, rate, rows, True)
    grad_values, grad_keys_local, head, sums, slopes, small = per_group(
        back_kernel,
        (
            grad_mixed,
            inputs,
            shifted,
            values,
            key_rows,
            rim,
            taps,
            rate,
            read,
            skip_row,
            entering,
            adjoint,
        ),
        ((rows, BF16), (rows, F32), (8, F32), (states, F32), (states, F32), (8, F32)),
        [pltpu.VMEM((rows * 8, LANES), F32), pltpu.VMEM((rows + 8, LANES), F32)],
        10 * element,
    )
    behind = lax.ppermute(head, "seq", [(s + 1, s) for s in range(count - 1)])
    padded = jnp.concatenate([jnp.zeros_like(behind), behind[:4]], 0)
    late = sum(taps[j] * padded[j : j + 8] for j in range(1, 4))
    grad_keys = jnp.concatenate(
        [grad_keys_local[: rows - 8], grad_keys_local[rows - 8 :] + late], 0
    ).astype(BF16)
    chunks.append(wires.scatter_sum(*by_tensor((mixed_in, grad_keys), (mixed_in, grad_values))))
    grad_normed = (
        back_product(grad_queries, w_query)
        + back_product(grad_keys, w_key)
        + back_product(grad_values, w_value)
    )
    grad_input_norm, d_gain_mix = norm_pull(grad_normed)
    d_tokens = (grad_hidden + grad_input_norm).astype(BF16).reshape(tokens.shape)

    extra = max(64, states - (-states) % 64)
    extra = 2 * extra
    filler = jnp.zeros((extra - states - 5, width), F32)
    few = jnp.zeros((extra - states - 2, width), F32)
    part_a = jnp.concatenate([sums, small[:5], filler], 0)
    part_b = jnp.concatenate([slopes, d_gain_mix[None], d_gain_ffn[None], few], 0)
    chunks.append(
        wires.scatter_sum(
            jnp.where(wires.core == 0, part_b, part_a), jnp.where(wires.core == 0, part_a, part_b)
        )
    )
    whole = [wires.halves(wires.gather(chunk)) for chunk in chunks]
    d_down = jnp.concatenate(whole[0] + whole[1], 0)
    d_up = jnp.concatenate(whole[2] + whole[3], 0)
    d_out, d_query = whole[4]
    d_key, d_value = whole[5]
    part_a, part_b = whole[6]
    sums, slopes = part_a[:states], part_b[:states]
    d_scale = gain_c * sums
    d_decay = read * slopes
    root = jnp.sqrt(-jnp.expm1(-2.0 * rate))
    d_rate = -jnp.exp(-rate) * d_decay + d_scale * gain_b * jnp.exp(-2.0 * rate) / root
    return (
        output.astype(BF16).reshape(tokens.shape),
        d_tokens,
        d_query,
        d_key,
        d_value,
        d_out,
        d_up,
        d_down,
        part_b[states],
        part_b[states + 1],
        part_a[states : states + 4],
        d_rate,
        d_scale * root,
        scale * sums,
        part_a[states + 4],
    )


def half_columns(value, which):
    columns = value.shape[1] // 2
    return lax.dynamic_slice_in_dim(value, which * columns, columns, 1)


def solution(mesh):
    split = P("batch", "seq", None)
    in_specs = (split,) + (P(),) * 13 + (split,)
    out_specs = (split, split) + (P(),) * 13
    return jax.shard_map(local, mesh=mesh, in_specs=in_specs, out_specs=out_specs, check_vma=False)
```

time: 1680 us -> 564 us (0.34)
  waiting for transfers between devices: 938 us -> 348 us
  local copies, waits for them, and re-layouts: 386 us -> 17.8 us
  matrix products: 177 us -> 25.9 us
  other arithmetic: 143 us -> 42.6 us
  starting transfers between devices: 7.67 us -> 77.2 us
  Pallas kernels: 0 us -> 40.2 us
    unnamed x13 -> x0, waiting for transfers between devices: 575 us -> none
    all_gather x9 -> x0, waiting for transfers between devices: 363 us -> none  [the longest x1 81.3 us: local(): lax.all_gather(partial_all[4], ('batch', 'seq'), axis=0, tiled=True)]
    ppermute x2 -> x87, waiting for transfers between devices: 0.01 us -> 348 us  [the longest x56 309 us: swap(): return lax.ppermute(value, ('batch', 'seq'), pairs)]
    dot_general x28 -> x25, matrix products: 177 us -> 25.9 us  [the longest x7 11.6 us: product(): return jnp.dot(left, right, preferred_element_type=F32)]
    pad x26 -> x0, local copies, waits for them, and re-layouts: 95.6 us -> none  [the longest x24 89.8 us: local_part(): states = lax.associative_scan(combine, (factor, ends), axis=0)[1]]
    reshape x18 -> x3, local copies, waits for them, and re-layouts: 74.2 us -> 0.7 us  [the longest x1 0.69 us: local(): skip_row = skip.reshape(1, width)]
    ppermute x2 -> x87, starting transfers between devices: 6.71 us -> 77.2 us  [the longest x56 53.8 us: swap(): return lax.ppermute(value, ('batch', 'seq'), pairs)]
    unnamed x275 -> x118, local copies, waits for them, and re-layouts: 64.5 us -> 12.9 us
  transfers between devices with their start and end apart: 13 -> 87, of which waited for: 8 -> 51; matrix products, arithmetic and copies ran while one was open for 22% -> 8% of each run, Pallas kernels for 0% -> 0%
where the time goes in v1:
time: 564 us; the launch traced here: 554 us
  waiting for transfers between devices  348 us (62%)
  starting transfers between devices  77.2 us (14%)
  other arithmetic  42.6 us (8%)
  Pallas kernels  40.2 us (7%)
  matrix products  25.9 us (5%)
  local copies, waits for them, and re-layouts  17.8 us (3%)
    ppermute x56, waiting for transfers between devices, swap(): return lax.ppermute(value, ('batch', 'seq'), pairs)  309 us
    ppermute x56, starting transfers between devices, swap(): return lax.ppermute(value, ('batch', 'seq'), pairs)  53.8 us
    pallas_call x4, Pallas kernels, per_group(): pl.pallas_call(kernel, grid=(width // LANES,), in_specs=[col_spec(x.shape...  40.2 us
    ppermute x8, waiting for transfers between devices, prefix(): arriving = lax.ppermute(total, 'seq', [(s, s ^ step) for s in range(count)])  32.1 us
    ppermute x8, starting transfers between devices, prefix(): arriving = lax.ppermute(total, 'seq', [(s, s ^ step) for s in range(count)])  13 us
    unnamed x118, local copies, waits for them, and re-layouts  12.9 us
    dot_general x7, matrix products, product(): return jnp.dot(left, right, preferred_element_type=F32)  11.6 us
    unnamed x15, other arithmetic  11.5 us
  transfers between devices with their start and end apart: 87, of which 51 were waited for; matrix products, arithmetic and copies ran while one was open for 8% of the time, Pallas kernels for 0%

profile of v1, /device:TPU:0, one launch (start us, length us, event | category | flops | bytes accessed | tf_op | source)
XLA Modules:
  0.0 553.9 jit_solution(40419642709992184)
XLA Ops:
  2.5 4.8 collective-permute-start
  10.5 4.2 shard_map.262
  18.0 5.0 collective-permute-done.1
  26.4 4.5 collective-permute-done.2
  35.1 3.5 collective-permute-done.3
  39.6 3.3 collective-permute-start.4
  44.8 3.9 collective-permute-done.4
  50.0 8.3 %shard_map.263 = (f32[256,768]{1,0:T(8,128)S(1)}, bf16[256,768]{1,0:T(8,128)(2,1)S(1)}) custom-call(f32[256,768]{1,0:T(8,128)S(1)} %copy-done.6, f32[256,768]{1,0:T(8,128)S(1)} %fusion.83.query_ref, f32[64,768]{1,0:T(8,128)S(1)} %add_select_fusion.3.enter_ref, f32[64,768]{1,0:T(8,128)S(1)} %copy-done.2, f32[64,768]{1,0:T(8,128)S(1)} %get-tuple-element.155.read_ref, ...), custom_call_target="tpu_custom_call" | custom-call | flops 50331648 | bytes 3345408 | tf_op jit(solution)/shard_map/pallas_call | solution.py:26
  61.0 3.2 multiply_convert_fusion
  64.3 2.9 fusion.6
  71.3 4.9 shard_map.264
  78.9 4.8 collective-permute-done.5
  88.0 3.5 collective-permute-done.6
  95.0 4.6 collective-permute-done.7
  101.3 4.6 fusion.8
  109.6 22.9 %shard_map.265 = (bf16[256,768]{1,0:T(8,128)(2,1)S(1)}, f32[256,768]{1,0:T(8,128)S(1)}, f32[8,768]{1,0:T(8,128)S(1)}, f32[64,768]{1,0:T(8,128)S(1)}, f32[64,768]{1,0:T(8,128)S(1)}, /*index=5*/f32[8,768]{1,0:T(8,128)S(1)}) custom-call(f32[256,768]{1,0:T(8,128)S(1)} %copy-done.13, f32[256,768]{1,0:T(8,128)S(1)} %copy-done.7, f32[256,768]{1,0:T(8,128)S(1)} %copy-done.11, ...), custom_call_target="tpu_custom_call" | custom-call | flops 125829120 | bytes 6380544 | tf_op jit(solution)/shard_map/pallas_call | solution.py:26
  134.9 3.3 collective-permute-done.9
  145.5 3.2 collective-permute-done.77
  148.7 2.5 collective-permute-start.78
  151.3 2.5 collective-permute-done.78
  155.3 2.7 collective-permute-done.79
  159.3 4.1 collective-permute-done.80
  164.1 4.0 collective-permute-done.81
  169.1 3.2 collective-permute-done.82
  179.3 3.5 collective-permute-done.84
  183.9 3.4 collective-permute-done.85
  203.7 4.6 collective-permute-done.66
  210.2 10.7 %collective-permute-done.55 = f32[384,768]{1,0:T(8,128)S(1)} collective-permute-done((f32[384,768]{1,0:T(8,128)S(1)}, f32[384,768]{1,0:T(8,128)S(1)}, u32[]{:S(2)}, u32[]{:S(2)}) %collective-permute-start.55) | collective-permute-done | bytes 1179680 | tf_op jit(solution)/shard_map/ppermute | solution.py:198
  223.2 16.7 %collective-permute-done.44 = f32[96,3072]{1,0:T(8,128)S(1)} collective-permute-done((f32[96,3072]{1,0:T(8,128)S(1)}, f32[96,3072]{1,0:T(8,128)S(1)}, u32[]{:S(2)}, u32[]{:S(2)}) %collective-permute-start.44) | collective-permute-done | bytes 1179680 | tf_op jit(solution)/shard_map/ppermute | solution.py:198
  242.2 16.7 %collective-permute-done.33 = f32[96,3072]{1,0:T(8,128)S(1)} collective-permute-done((f32[96,3072]{1,0:T(8,128)S(1)}, f32[96,3072]{1,0:T(8,128)S(1)}, u32[]{:S(2)}, u32[]{:S(2)}) %collective-permute-start.33) | collective-permute-done | bytes 1179680 | tf_op jit(solution)/shard_map/ppermute | solution.py:198
  261.1 16.7 %collective-permute-done.11 = f32[384,768]{1,0:T(8,128)S(1)} collective-permute-done((f32[384,768]{1,0:T(8,128)S(1)}, f32[384,768]{1,0:T(8,128)S(1)}, u32[]{:S(2)}, u32[]{:S(2)}) %collective-permute-start.11) | collective-permute-done | bytes 1179680 | tf_op jit(solution)/shard_map/ppermute | solution.py:198
  282.6 11.6 %collective-permute-done.34 = f32[48,3072]{1,0:T(8,128)S(1)} collective-permute-done((f32[48,3072]{1,0:T(8,128)S(1)}, f32[48,3072]{1,0:T(8,128)S(1)}, u32[]{:S(2)}, u32[]{:S(2)}) %collective-permute-start.34) | collective-permute-done | bytes 589856 | tf_op jit(solution)/shard_map/ppermute | solution.py:198
  294.4 8.2 %collective-permute-done.12 = f32[192,768]{1,0:T(8,128)S(1)} collective-permute-done((f32[192,768]{1,0:T(8,128)S(1)}, f32[192,768]{1,0:T(8,128)S(1)}, u32[]{:S(2)}, u32[]{:S(2)}) %collective-permute-start.12) | collective-permute-done | bytes 589856 | tf_op jit(solution)/shard_map/ppermute | solution.py:198
  306.9 3.0 collective-permute-start.58
  309.9 8.8 %collective-permute-done.35 = f32[24,3072]{1,0:T(8,128)S(1)} collective-permute-done((f32[24,3072]{1,0:T(8,128)S(1)}, f32[24,3072]{1,0:T(8,128)S(1)}, u32[]{:S(2)}, u32[]{:S(2)}) %collective-permute-start.35) | collective-permute-done | bytes 294944 | tf_op jit(solution)/shard_map/ppermute | solution.py:198
  318.9 5.7 %collective-permute-done.13 = f32[96,768]{1,0:T(8,128)S(1)} collective-permute-done((f32[96,768]{1,0:T(8,128)S(1)}, f32[96,768]{1,0:T(8,128)S(1)}, u32[]{:S(2)}, u32[]{:S(2)}) %collective-permute-start.13) | collective-permute-done | bytes 294944 | tf_op jit(solution)/shard_map/ppermute | solution.py:198
  325.0 2.6 collective-permute-start.14
  328.1 16.0 %collective-permute-done.47 = f32[12,3072]{1,0:T(8,128)S(1)} collective-permute-done((f32[12,3072]{1,0:T(8,128)S(1)}, f32[12,3072]{1,0:T(8,128)S(1)}, u32[]{:S(2)}, u32[]{:S(2)}) %collective-permute-start.47) | collective-permute-done | bytes 147488 | tf_op jit(solution)/shard_map/ppermute | solution.py:198
  344.1 7.3 %collective-permute-done.36 = f32[12,3072]{1,0:T(8,128)S(1)} collective-permute-done((f32[12,3072]{1,0:T(8,128)S(1)}, f32[12,3072]{1,0:T(8,128)S(1)}, u32[]{:S(2)}, u32[]{:S(2)}) %collective-permute-start.36) | collective-permute-done | bytes 147488 | tf_op jit(solution)/shard_map/ppermute | solution.py:198
  351.5 11.5 %collective-permute-done.14 = f32[48,768]{1,0:T(8,128)S(1)} collective-permute-done((f32[48,768]{1,0:T(8,128)S(1)}, f32[48,768]{1,0:T(8,128)S(1)}, u32[]{:S(2)}, u32[]{:S(2)}) %collective-permute-start.14) | collective-permute-done | bytes 147488 | tf_op jit(solution)/shard_map/ppermute | solution.py:198
  363.1 6.3 %collective-permute-done.70 = f32[48,768]{1,0:T(8,128)S(1)} collective-permute-done((f32[48,768]{1,0:T(8,128)S(1)}, f32[48,768]{1,0:T(8,128)S(1)}, u32[]{:S(2)}, u32[]{:S(2)}) %collective-permute-start.70) | collective-permute-done | bytes 147488 | tf_op jit(solution)/shard_map/ppermute | solution.py:198
  369.4 3.1 collective-permute-done.59
  372.6 4.3 collective-permute-done.48
  376.9 4.1 collective-permute-done.37
  381.1 3.0 collective-permute-done.15
  386.3 4.1 collective-permute-done.71
  390.5 6.2 %collective-permute-done.60 = f32[96,768]{1,0:T(8,128)S(1)} collective-permute-done((f32[96,768]{1,0:T(8,128)S(1)}, f32[96,768]{1,0:T(8,128)S(1)}, u32[]{:S(2)}, u32[]{:S(2)}) %collective-permute-start.60) | collective-permute-done | bytes 294944 | tf_op jit(solution)/shard_map/ppermute | solution.py:198
  396.8 6.2 %collective-permute-done.49 = f32[24,3072]{1,0:T(8,128)S(1)} collective-permute-done((f32[24,3072]{1,0:T(8,128)S(1)}, f32[24,3072]{1,0:T(8,128)S(1)}, u32[]{:S(2)}, u32[]{:S(2)}) %collective-permute-start.49) | collective-permute-done | bytes 294944 | tf_op jit(solution)/shard_map/ppermute | solution.py:198
  403.2 6.2 %collective-permute-done.38 = f32[24,3072]{1,0:T(8,128)S(1)} collective-permute-done((f32[24,3072]{1,0:T(8,128)S(1)}, f32[24,3072]{1,0:T(8,128)S(1)}, u32[]{:S(2)}, u32[]{:S(2)}) %collective-permute-start.38) | collective-permute-done | bytes 294944 | tf_op jit(solution)/shard_map/ppermute | solution.py:198
  409.4 12.5 %collective-permute-done.24 = f32[96,768]{1,0:T(8,128)S(1)} collective-permute-done((f32[96,768]{1,0:T(8,128)S(1)}, f32[96,768]{1,0:T(8,128)S(1)}, u32[]{:S(2)}, u32[]{:S(2)}) %collective-permute-start.24) | collective-permute-done | bytes 294944 | tf_op jit(solution)/shard_map/ppermute | solution.py:198
  422.1 8.7 %collective-permute-done.25 = f32[48,768]{1,0:T(8,128)S(1)} collective-permute-done((f32[48,768]{1,0:T(8,128)S(1)}, f32[48,768]{1,0:T(8,128)S(1)}, u32[]{:S(2)}, u32[]{:S(2)}) %collective-permute-start.25) | collective-permute-done | bytes 147488 | tf_op jit(solution)/shard_map/ppermute | solution.py:198
  431.1 8.5 %collective-permute-done.26 = f32[48,768]{1,0:T(8,128)S(1)} collective-permute-done((f32[48,768]{1,0:T(8,128)S(1)}, f32[48,768]{1,0:T(8,128)S(1)}, u32[]{:S(2)}, u32[]{:S(2)}) %collective-permute-start.26) | collective-permute-done | bytes 147488 | tf_op jit(solution)/shard_map/ppermute | solution.py:198
  439.6 2.5 collective-permute-start.17
  445.1 4.0 collective-permute-done.27
  450.9 5.2 collective-permute-done.17
  458.3 9.7 %collective-permute-done.40 = f32[96,3072]{1,0:T(8,128)S(1)} collective-permute-done((f32[96,3072]{1,0:T(8,128)S(1)}, f32[96,3072]{1,0:T(8,128)S(1)}, u32[]{:S(2)}, u32[]{:S(2)}) %collective-permute-start.40) | collective-permute-done | bytes 1179680 | tf_op jit(solution)/shard_map/ppermute | solution.py:198
  468.2 4.3 collective-permute-done.28
  472.7 20.5 %collective-permute-done.62 = f32[384,768]{1,0:T(8,128)S(1)} collective-permute-done((f32[384,768]{1,0:T(8,128)S(1)}, f32[384,768]{1,0:T(8,128)S(1)}, u32[]{:S(2)}, u32[]{:S(2)}) %collective-permute-start.62) | collective-permute-done | bytes 1179680 | tf_op jit(solution)/shard_map/ppermute | solution.py:198
  496.6 13.1 %collective-permute-done.51 = f32[96,3072]{1,0:T(8,128)S(1)} collective-permute-done((f32[96,3072]{1,0:T(8,128)S(1)}, f32[96,3072]{1,0:T(8,128)S(1)}, u32[]{:S(2)}, u32[]{:S(2)}) %collective-permute-start.51) | collective-permute-done | bytes 1179680 | tf_op jit(solution)/shard_map/ppermute | solution.py:198
  519.3 6.6 %collective-permute-done.19 = f32[384,768]{1,0:T(8,128)S(1)} collective-permute-done((f32[384,768]{1,0:T(8,128)S(1)}, f32[384,768]{1,0:T(8,128)S(1)}, u32[]{:S(2)}, u32[]{:S(2)}) %collective-permute-start.19) | collective-permute-done | bytes 1179680 | tf_op jit(solution)/shard_map/ppermute | solution.py:198
  525.8 12.6 %collective-permute-done.29 = f32[384,768]{1,0:T(8,128)S(1)} collective-permute-done((f32[384,768]{1,0:T(8,128)S(1)}, f32[384,768]{1,0:T(8,128)S(1)}, u32[]{:S(2)}, u32[]{:S(2)}) %collective-permute-start.29) | collective-permute-done | bytes 1179680 | tf_op jit(solution)/shard_map/ppermute | solution.py:198
  543.3 2.5 pad_maximum_fusion
  547.9 3.3 copy-done.43
  551.2 2.5 pad_maximum_fusion.1
  (402 shorter events, 130.4 us)
Async XLA Ops:
  39.6 9.1 %collective-permute-start.4 = (f32[64,768]{1,0:T(8,128)S(1)}, f32[64,768]{1,0:T(8,128)S(1)}, u32[]{:S(2)}, u32[]{:S(2)}) collective-permute-start(f32[64,768]{1,0:T(8,128)S(1)} %select_add_fusion.3), channel_id=1, source_target_pairs={{0,8},{1,9},{2,10},{3,11},{4,12},{5,13},{6,14},{7,15},{8,0},{9,1},... | collective-permute-start | bytes 589832 | tf_op jit(solution)/shard_map/ppermute | solution.py:252
  99.6 8.7 %collective-permute-start.8 = (f32[64,768]{1,0:T(8,128)S(1)}, f32[64,768]{1,0:T(8,128)S(1)}, u32[]{:S(2)}, u32[]{:S(2)}) collective-permute-start(f32[64,768]{1,0:T(8,128)S(1)} %select_add_fusion), channel_id=1, source_target_pairs={{0,8},{1,9},{2,10},{3,11},{4,12},{5,13},{6,14},{7,15},{8,0},{9,1},... | collective-permute-start | bytes 589832 | tf_op jit(solution)/shard_map/ppermute | solution.py:252
  151.2 37.1 %collective-permute-start.65 = (f32[768,768]{1,0:T(8,128)S(1)}, f32[768,768]{1,0:T(8,128)S(1)}, u32[]{:S(2)}, u32[]{:S(2)}) collective-permute-start(f32[768,768]{1,0:T(8,128)S(1)} %fusion.11), channel_id=1, source_target_pairs={{0,16},{16,0},{1,17},{17,1},{2,18},{18,2},{3,19},{19,3},{4,20},{20... | collective-permute-start | bytes 7077896 | tf_op jit(solution)/shard_map/ppermute | solution.py:201
  174.5 17.5 %collective-permute-start.54 = (f32[768,768]{1,0:T(8,128)S(1)}, f32[768,768]{1,0:T(8,128)S(1)}, u32[]{:S(2)}, u32[]{:S(2)}) collective-permute-start(f32[768,768]{1,0:T(8,128)S(1)} %fusion.15), channel_id=1, source_target_pairs={{0,16},{16,0},{1,17},{17,1},{2,18},{18,2},{3,19},{19,3},{4,20},{20... | collective-permute-start | bytes 7077896 | tf_op jit(solution)/shard_map/ppermute | solution.py:201
  174.6 19.5 %collective-permute-start.43 = (f32[192,3072]{1,0:T(8,128)S(1)}, f32[192,3072]{1,0:T(8,128)S(1)}, u32[]{:S(2)}, u32[]{:S(2)}) collective-permute-start(f32[192,3072]{1,0:T(8,128)S(1)} %fusion.45), channel_id=1, source_target_pairs={{0,16},{16,0},{1,17},{17,1},{2,18},{18,2},{3,19},{19,3},{4,20},{20... | collective-permute-start | bytes 7077896 | tf_op jit(solution)/shard_map/ppermute | solution.py:201
  182.8 11.9 %collective-permute-start.32 = (f32[192,3072]{1,0:T(8,128)S(1)}, f32[192,3072]{1,0:T(8,128)}, u32[]{:S(2)}, u32[]{:S(2)}) collective-permute-start(f32[192,3072]{1,0:T(8,128)S(1)} %fusion.49), channel_id=1, source_target_pairs={{0,16},{16,0},{1,17},{17,1},{2,18},{18,2},{3,19},{19,3},{4,20},{20... | collective-permute-start | bytes 7077896 | tf_op jit(solution)/shard_map/ppermute | solution.py:201
  187.3 11.3 %collective-permute-start.10 = (f32[768,768]{1,0:T(8,128)S(1)}, f32[768,768]{1,0:T(8,128)S(1)}, u32[]{:S(2)}, u32[]{:S(2)}) collective-permute-start(f32[768,768]{1,0:T(8,128)S(1)} %fusion.31), channel_id=1, source_target_pairs={{0,16},{16,0},{1,17},{17,1},{2,18},{18,2},{3,19},{19,3},{4,20},{20... | collective-permute-start | bytes 7077896 | tf_op jit(solution)/shard_map/ppermute | solution.py:201
  188.3 13.1 %collective-permute-start.21 = (f32[768,768]{1,0:T(8,128)S(1)}, f32[768,768]{1,0:T(8,128)S(1)}, u32[]{:S(2)}, u32[]{:S(2)}) collective-permute-start(f32[768,768]{1,0:T(8,128)S(1)} %fusion.27), channel_id=1, source_target_pairs={{0,16},{16,0},{1,17},{17,1},{2,18},{18,2},{3,19},{19,3},{4,20},{20... | collective-permute-start | bytes 7077896 | tf_op jit(solution)/shard_map/ppermute | solution.py:201
  192.0 16.3 %collective-permute-start.66 = (f32[384,768]{1,0:T(8,128)S(1)}, f32[384,768]{1,0:T(8,128)S(1)}, u32[]{:S(2)}, u32[]{:S(2)}) collective-permute-start(f32[384,768]{1,0:T(8,128)S(1)} %get-tuple-element.58), channel_id=1, source_target_pairs={{0,1},{1,0},{2,3},{3,2},{4,5},{5,4},{6,7},{7,6},{8,9},{9,8},{10,11... | collective-permute-start | bytes 3538952 | tf_op jit(solution)/shard_map/ppermute | solution.py:198
  194.2 26.8 %collective-permute-start.55 = (f32[384,768]{1,0:T(8,128)S(1)}, f32[384,768]{1,0:T(8,128)S(1)}, u32[]{:S(2)}, u32[]{:S(2)}) collective-permute-start(f32[384,768]{1,0:T(8,128)S(1)} %get-tuple-element.60), channel_id=1, source_target_pairs={{0,1},{1,0},{2,3},{3,2},{4,5},{5,4},{6,7},{7,6},{8,9},{9,8},{10,11... | collective-permute-start | bytes 3538952 | tf_op jit(solution)/shard_map/ppermute | solution.py:198
  194.8 45.1 %collective-permute-start.44 = (f32[96,3072]{1,0:T(8,128)S(1)}, f32[96,3072]{1,0:T(8,128)S(1)}, u32[]{:S(2)}, u32[]{:S(2)}) collective-permute-start(f32[96,3072]{1,0:T(8,128)S(1)} %get-tuple-element.62), channel_id=1, source_target_pairs={{0,1},{1,0},{2,3},{3,2},{4,5},{5,4},{6,7},{7,6},{8,9},{9,8},{10,11... | collective-permute-start | bytes 3538952 | tf_op jit(solution)/shard_map/ppermute | solution.py:198
  198.6 60.3 %collective-permute-start.33 = (f32[96,3072]{1,0:T(8,128)S(1)}, f32[96,3072]{1,0:T(8,128)S(1)}, u32[]{:S(2)}, u32[]{:S(2)}) collective-permute-start(f32[96,3072]{1,0:T(8,128)S(1)} %get-tuple-element.64), channel_id=1, source_target_pairs={{0,1},{1,0},{2,3},{3,2},{4,5},{5,4},{6,7},{7,6},{8,9},{9,8},{10,11... | collective-permute-start | bytes 3538952 | tf_op jit(solution)/shard_map/ppermute | solution.py:198
  201.4 76.4 %collective-permute-start.11 = (f32[384,768]{1,0:T(8,128)S(1)}, f32[384,768]{1,0:T(8,128)S(1)}, u32[]{:S(2)}, u32[]{:S(2)}) collective-permute-start(f32[384,768]{1,0:T(8,128)S(1)} %get-tuple-element.76), channel_id=1, source_target_pairs={{0,1},{1,0},{2,3},{3,2},{4,5},{5,4},{6,7},{7,6},{8,9},{9,8},{10,11... | collective-permute-start | bytes 3538952 | tf_op jit(solution)/shard_map/ppermute | solution.py:198
  208.3 94.5 %collective-permute-start.22 = (f32[384,768]{1,0:T(8,128)S(1)}, f32[384,768]{1,0:T(8,128)S(1)}, u32[]{:S(2)}, u32[]{:S(2)}) collective-permute-start(f32[384,768]{1,0:T(8,128)S(1)} %get-tuple-element.74), channel_id=1, source_target_pairs={{0,1},{1,0},{2,3},{3,2},{4,5},{5,4},{6,7},{7,6},{8,9},{9,8},{10,11... | collective-permute-start | bytes 3538952 | tf_op jit(solution)/shard_map/ppermute | solution.py:198
  220.9 59.1 %collective-permute-start.67 = (f32[192,768]{1,0:T(8,128)S(1)}, f32[192,768]{1,0:T(8,128)S(1)}, u32[]{:S(2)}, u32[]{:S(2)}) collective-permute-start(f32[192,768]{1,0:T(8,128)S(1)} %get-tuple-element.78), channel_id=1, source_target_pairs={{0,2},{1,3},{2,0},{3,1},{4,6},{5,7},{6,4},{7,5},{8,10},{9,11},{10,... | collective-permute-start | bytes 1769480 | tf_op jit(solution)/shard_map/ppermute | solution.py:198
  239.9 40.4 %collective-permute-start.56 = (f32[192,768]{1,0:T(8,128)S(1)}, f32[192,768]{1,0:T(8,128)S(1)}, u32[]{:S(2)}, u32[]{:S(2)}) collective-permute-start(f32[192,768]{1,0:T(8,128)S(1)} %get-tuple-element.80), channel_id=1, source_target_pairs={{0,2},{1,3},{2,0},{3,1},{4,6},{5,7},{6,4},{7,5},{8,10},{9,11},{10,... | collective-permute-start | bytes 1769480 | tf_op jit(solution)/shard_map/ppermute | solution.py:198
  258.8 21.7 %collective-permute-start.45 = (f32[48,3072]{1,0:T(8,128)S(1)}, f32[48,3072]{1,0:T(8,128)S(1)}, u32[]{:S(2)}, u32[]{:S(2)}) collective-permute-start(f32[48,3072]{1,0:T(8,128)S(1)} %get-tuple-element.82), channel_id=1, source_target_pairs={{0,2},{1,3},{2,0},{3,1},{4,6},{5,7},{6,4},{7,5},{8,10},{9,11},{10,... | collective-permute-start | bytes 1769480 | tf_op jit(solution)/shard_map/ppermute | solution.py:198
  277.8 16.3 %collective-permute-start.34 = (f32[48,3072]{1,0:T(8,128)S(1)}, f32[48,3072]{1,0:T(8,128)S(1)}, u32[]{:S(2)}, u32[]{:S(2)}) collective-permute-start(f32[48,3072]{1,0:T(8,128)S(1)} %get-tuple-element.84), channel_id=1, source_target_pairs={{0,2},{1,3},{2,0},{3,1},{4,6},{5,7},{6,4},{7,5},{8,10},{9,11},{10,... | collective-permute-start | bytes 1769480 | tf_op jit(solution)/shard_map/ppermute | solution.py:198
  280.1 22.5 %collective-permute-start.12 = (f32[192,768]{1,0:T(8,128)S(1)}, f32[192,768]{1,0:T(8,128)S(1)}, u32[]{:S(2)}, u32[]{:S(2)}) collective-permute-start(f32[192,768]{1,0:T(8,128)S(1)} %get-tuple-element.88), channel_id=1, source_target_pairs={{0,2},{1,3},{2,0},{3,1},{4,6},{5,7},{6,4},{7,5},{8,10},{9,11},{10,... | collective-permute-start | bytes 1769480 | tf_op jit(solution)/shard_map/ppermute | solution.py:198
  280.3 24.7 %collective-permute-start.68 = (f32[96,768]{1,0:T(8,128)S(1)}, f32[96,768]{1,0:T(8,128)S(1)}, u32[]{:S(2)}, u32[]{:S(2)}) collective-permute-start(f32[96,768]{1,0:T(8,128)S(1)} %get-tuple-element.94), channel_id=1, source_target_pairs={{0,4},{1,5},{2,6},{3,7},{4,0},{5,1},{6,2},{7,3},{8,12},{9,13},{10,... | collective-permute-start | bytes 884744 | tf_op jit(solution)/shard_map/ppermute | solution.py:198
  280.6 26.2 %collective-permute-start.57 = (f32[96,768]{1,0:T(8,128)S(1)}, f32[96,768]{1,0:T(8,128)S(1)}, u32[]{:S(2)}, u32[]{:S(2)}) collective-permute-start(f32[96,768]{1,0:T(8,128)S(1)} %get-tuple-element.98), channel_id=1, source_target_pairs={{0,4},{1,5},{2,6},{3,7},{4,0},{5,1},{6,2},{7,3},{8,12},{9,13},{10,... | collective-permute-start | bytes 884744 | tf_op jit(solution)/shard_map/ppermute | solution.py:198
  294.2 12.8 %collective-permute-start.46 = (f32[24,3072]{1,0:T(8,128)S(1)}, f32[24,3072]{1,0:T(8,128)S(1)}, u32[]{:S(2)}, u32[]{:S(2)}) collective-permute-start(f32[24,3072]{1,0:T(8,128)S(1)} %get-tuple-element.102), channel_id=1, source_target_pairs={{0,4},{1,5},{2,6},{3,7},{4,0},{5,1},{6,2},{7,3},{8,12},{9,13},{10,... | collective-permute-start | bytes 884744 | tf_op jit(solution)/shard_map/ppermute | solution.py:198
  302.6 16.2 %collective-permute-start.35 = (f32[24,3072]{1,0:T(8,128)S(1)}, f32[24,3072]{1,0:T(8,128)S(1)}, u32[]{:S(2)}, u32[]{:S(2)}) collective-permute-start(f32[24,3072]{1,0:T(8,128)S(1)} %get-tuple-element.106), channel_id=1, source_target_pairs={{0,4},{1,5},{2,6},{3,7},{4,0},{5,1},{6,2},{7,3},{8,12},{9,13},{10,... | collective-permute-start | bytes 884744 | tf_op jit(solution)/shard_map/ppermute | solution.py:198
  302.8 21.8 %collective-permute-start.13 = (f32[96,768]{1,0:T(8,128)S(1)}, f32[96,768]{1,0:T(8,128)S(1)}, u32[]{:S(2)}, u32[]{:S(2)}) collective-permute-start(f32[96,768]{1,0:T(8,128)S(1)} %get-tuple-element.114), channel_id=1, source_target_pairs={{0,4},{1,5},{2,6},{3,7},{4,0},{5,1},{6,2},{7,3},{8,12},{9,13},{10,... | collective-permute-start | bytes 884744 | tf_op jit(solution)/shard_map/ppermute | solution.py:198
  305.0 79.2 %collective-permute-start.23 = (f32[192,768]{1,0:T(8,128)S(1)}, f32[192,768]{1,0:T(8,128)S(1)}, u32[]{:S(2)}, u32[]{:S(2)}) collective-permute-start(f32[192,768]{1,0:T(8,128)S(1)} %get-tuple-element.86), channel_id=1, source_target_pairs={{0,2},{1,3},{2,0},{3,1},{4,6},{5,7},{6,4},{7,5},{8,10},{9,11},{10,... | collective-permute-start | bytes 1769480 | tf_op jit(solution)/shard_map/ppermute | solution.py:198
  306.8 18.1 %collective-permute-start.69 = (f32[48,768]{1,0:T(8,128)S(1)}, f32[48,768]{1,0:T(8,128)S(1)}, u32[]{:S(2)}, u32[]{:S(2)}) collective-permute-start(f32[48,768]{1,0:T(8,128)S(1)} %dynamic-slice_add_fusion.40), channel_id=1, source_target_pairs={{0,8},{1,9},{2,10},{3,11},{4,12},{5,13},{6,14},{7,15},{8,0},{9,1},... | collective-permute-start | bytes 442376 | tf_op jit(solution)/shard_map/ppermute | solution.py:198
  306.9 20.7 %collective-permute-start.58 = (f32[48,768]{1,0:T(8,128)S(1)}, f32[48,768]{1,0:T(8,128)S(1)}, u32[]{:S(2)}, u32[]{:S(2)}) collective-permute-start(f32[48,768]{1,0:T(8,128)S(1)} %dynamic-slice_add_fusion.41), channel_id=1, source_target_pairs={{0,8},{1,9},{2,10},{3,11},{4,12},{5,13},{6,14},{7,15},{8,0},{9,1},... | collective-permute-start | bytes 442376 | tf_op jit(solution)/shard_map/ppermute | solution.py:198
  318.8 25.3 %collective-permute-start.47 = (f32[12,3072]{1,0:T(8,128)S(1)}, f32[12,3072]{1,0:T(8,128)S(1)}, u32[]{:S(2)}, u32[]{:S(2)}) collective-permute-start(f32[12,3072]{1,0:T(8,128)S(1)} %dynamic-slice_add_fusion.38), channel_id=1, source_target_pairs={{0,8},{1,9},{2,10},{3,11},{4,12},{5,13},{6,14},{7,15},{8,0},{9,1},... | collective-permute-start | bytes 442376 | tf_op jit(solution)/shard_map/ppermute | solution.py:198
  324.6 26.9 %collective-permute-start.36 = (f32[12,3072]{1,0:T(8,128)S(1)}, f32[12,3072]{1,0:T(8,128)S(1)}, u32[]{:S(2)}, u32[]{:S(2)}) collective-permute-start(f32[12,3072]{1,0:T(8,128)S(1)} %dynamic-slice_add_fusion.39), channel_id=1, source_target_pairs={{0,8},{1,9},{2,10},{3,11},{4,12},{5,13},{6,14},{7,15},{8,0},{9,1},... | collective-permute-start | bytes 442376 | tf_op jit(solution)/shard_map/ppermute | solution.py:198
  325.0 38.1 %collective-permute-start.14 = (f32[48,768]{1,0:T(8,128)S(1)}, f32[48,768]{1,0:T(8,128)S(1)}, u32[]{:S(2)}, u32[]{:S(2)}) collective-permute-start(f32[48,768]{1,0:T(8,128)S(1)} %dynamic-slice_add_fusion.43), channel_id=1, source_target_pairs={{0,8},{1,9},{2,10},{3,11},{4,12},{5,13},{6,14},{7,15},{8,0},{9,1},... | collective-permute-start | bytes 442376 | tf_op jit(solution)/shard_map/ppermute | solution.py:198
  327.6 41.7 %collective-permute-start.70 = (f32[48,768]{1,0:T(8,128)S(1)}, f32[48,768]{1,0:T(8,128)S(1)}, u32[]{:S(2)}, u32[]{:S(2)}) collective-permute-start(f32[48,768]{1,0:T(8,128)S(1)} %add_add_fusion.5), channel_id=1, source_target_pairs={{0,8},{1,9},{2,10},{3,11},{4,12},{5,13},{6,14},{7,15},{8,0},{9,1},... | collective-permute-start | bytes 442376 | tf_op jit(solution)/shard_map/ppermute | solution.py:198
  344.1 28.4 %collective-permute-start.59 = (f32[48,768]{1,0:T(8,128)S(1)}, f32[48,768]{1,0:T(8,128)S(1)}, u32[]{:S(2)}, u32[]{:S(2)}) collective-permute-start(f32[48,768]{1,0:T(8,128)S(1)} %add_add_fusion.6), channel_id=1, source_target_pairs={{0,8},{1,9},{2,10},{3,11},{4,12},{5,13},{6,14},{7,15},{8,0},{9,1},... | collective-permute-start | bytes 442376 | tf_op jit(solution)/shard_map/ppermute | solution.py:198
  351.4 25.4 %collective-permute-start.48 = (f32[12,3072]{1,0:T(8,128)S(1)}, f32[12,3072]{1,0:T(8,128)S(1)}, u32[]{:S(2)}, u32[]{:S(2)}) collective-permute-start(f32[12,3072]{1,0:T(8,128)S(1)} %add_add_fusion.3), channel_id=1, source_target_pairs={{0,8},{1,9},{2,10},{3,11},{4,12},{5,13},{6,14},{7,15},{8,0},{9,1},... | collective-permute-start | bytes 442376 | tf_op jit(solution)/shard_map/ppermute | solution.py:198
  363.0 18.0 %collective-permute-start.37 = (f32[12,3072]{1,0:T(8,128)S(1)}, f32[12,3072]{1,0:T(8,128)S(1)}, u32[]{:S(2)}, u32[]{:S(2)}) collective-permute-start(f32[12,3072]{1,0:T(8,128)S(1)} %add_add_fusion.4), channel_id=1, source_target_pairs={{0,8},{1,9},{2,10},{3,11},{4,12},{5,13},{6,14},{7,15},{8,0},{9,1},... | collective-permute-start | bytes 442376 | tf_op jit(solution)/shard_map/ppermute | solution.py:198
  369.3 14.8 %collective-permute-start.15 = (f32[48,768]{1,0:T(8,128)S(1)}, f32[48,768]{1,0:T(8,128)S(1)}, u32[]{:S(2)}, u32[]{:S(2)}) collective-permute-start(f32[48,768]{1,0:T(8,128)S(1)} %add_add_fusion.8), channel_id=1, source_target_pairs={{0,8},{1,9},{2,10},{3,11},{4,12},{5,13},{6,14},{7,15},{8,0},{9,1},... | collective-permute-start | bytes 442376 | tf_op jit(solution)/shard_map/ppermute | solution.py:198
  372.5 17.9 %collective-permute-start.71 = (f32[96,768]{1,0:T(8,128)S(1)}, f32[96,768]{1,0:T(8,128)S(1)}, u32[]{:S(2)}, u32[]{:S(2)}) collective-permute-start(f32[96,768]{1,0:T(8,128)S(1)} %pad_maximum_fusion.22), channel_id=1, source_target_pairs={{0,4},{1,5},{2,6},{3,7},{4,0},{5,1},{6,2},{7,3},{8,12},{9,13},{10,... | collective-permute-start | bytes 884744 | tf_op jit(solution)/shard_map/ppermute | solution.py:198
  376.8 19.9 %collective-permute-start.60 = (f32[96,768]{1,0:T(8,128)S(1)}, f32[96,768]{1,0:T(8,128)S(1)}, u32[]{:S(2)}, u32[]{:S(2)}) collective-permute-start(f32[96,768]{1,0:T(8,128)S(1)} %pad_maximum_fusion.21), channel_id=1, source_target_pairs={{0,4},{1,5},{2,6},{3,7},{4,0},{5,1},{6,2},{7,3},{8,12},{9,13},{10,... | collective-permute-start | bytes 884744 | tf_op jit(solution)/shard_map/ppermute | solution.py:198
  381.0 22.0 %collective-permute-start.49 = (f32[24,3072]{1,0:T(8,128)S(1)}, f32[24,3072]{1,0:T(8,128)S(1)}, u32[]{:S(2)}, u32[]{:S(2)}) collective-permute-start(f32[24,3072]{1,0:T(8,128)S(1)} %pad_maximum_fusion.20), channel_id=1, source_target_pairs={{0,4},{1,5},{2,6},{3,7},{4,0},{5,1},{6,2},{7,3},{8,12},{9,13},{10,... | collective-permute-start | bytes 884744 | tf_op jit(solution)/shard_map/ppermute | solution.py:198
  384.1 25.3 %collective-permute-start.38 = (f32[24,3072]{1,0:T(8,128)S(1)}, f32[24,3072]{1,0:T(8,128)S(1)}, u32[]{:S(2)}, u32[]{:S(2)}) collective-permute-start(f32[24,3072]{1,0:T(8,128)S(1)} %pad_maximum_fusion.19), channel_id=1, source_target_pairs={{0,4},{1,5},{2,6},{3,7},{4,0},{5,1},{6,2},{7,3},{8,12},{9,13},{10,... | collective-permute-start | bytes 884744 | tf_op jit(solution)/shard_map/ppermute | solution.py:198
  384.2 46.8 %collective-permute-start.16 = (f32[96,768]{1,0:T(8,128)S(1)}, f32[96,768]{1,0:T(8,128)S(1)}, u32[]{:S(2)}, u32[]{:S(2)}) collective-permute-start(f32[96,768]{1,0:T(8,128)S(1)} %pad_maximum_fusion.17), channel_id=1, source_target_pairs={{0,4},{1,5},{2,6},{3,7},{4,0},{5,1},{6,2},{7,3},{8,12},{9,13},{10,... | collective-permute-start | bytes 884744 | tf_op jit(solution)/shard_map/ppermute | solution.py:198
  390.4 31.5 %collective-permute-start.24 = (f32[96,768]{1,0:T(8,128)S(1)}, f32[96,768]{1,0:T(8,128)S(1)}, u32[]{:S(2)}, u32[]{:S(2)}) collective-permute-start(f32[96,768]{1,0:T(8,128)S(1)} %get-tuple-element.110), channel_id=1, source_target_pairs={{0,4},{1,5},{2,6},{3,7},{4,0},{5,1},{6,2},{7,3},{8,12},{9,13},{10,... | collective-permute-start | bytes 884744 | tf_op jit(solution)/shard_map/ppermute | solution.py:198
  396.7 46.4 %collective-permute-start.72 = (f32[192,768]{1,0:T(8,128)S(1)}, f32[192,768]{1,0:T(8,128)S(1)}, u32[]{:S(2)}, u32[]{:S(2)}) collective-permute-start(f32[192,768]{1,0:T(8,128)S(1)} %pad_maximum_fusion.15), channel_id=1, source_target_pairs={{0,2},{1,3},{2,0},{3,1},{4,6},{5,7},{6,4},{7,5},{8,10},{9,11},{10,... | collective-permute-start | bytes 1769480 | tf_op jit(solution)/shard_map/ppermute | solution.py:198
  403.0 40.3 %collective-permute-start.61 = (f32[192,768]{1,0:T(8,128)S(1)}, f32[192,768]{1,0:T(8,128)S(1)}, u32[]{:S(2)}, u32[]{:S(2)}) collective-permute-start(f32[192,768]{1,0:T(8,128)S(1)} %pad_maximum_fusion.14), channel_id=1, source_target_pairs={{0,2},{1,3},{2,0},{3,1},{4,6},{5,7},{6,4},{7,5},{8,10},{9,11},{10,... | collective-permute-start | bytes 1769480 | tf_op jit(solution)/shard_map/ppermute | solution.py:198
  409.4 33.0 %collective-permute-start.50 = (f32[48,3072]{1,0:T(8,128)S(1)}, f32[48,3072]{1,0:T(8,128)S(1)}, u32[]{:S(2)}, u32[]{:S(2)}) collective-permute-start(f32[48,3072]{1,0:T(8,128)S(1)} %pad_maximum_fusion.13), channel_id=1, source_target_pairs={{0,2},{1,3},{2,0},{3,1},{4,6},{5,7},{6,4},{7,5},{8,10},{9,11},{10,... | collective-permute-start | bytes 1769480 | tf_op jit(solution)/shard_map/ppermute | solution.py:198
  421.9 8.9 %collective-permute-start.25 = (f32[48,768]{1,0:T(8,128)S(1)}, f32[48,768]{1,0:T(8,128)S(1)}, u32[]{:S(2)}, u32[]{:S(2)}) collective-permute-start(f32[48,768]{1,0:T(8,128)S(1)} %dynamic-slice_add_fusion.42), channel_id=1, source_target_pairs={{0,8},{1,9},{2,10},{3,11},{4,12},{5,13},{6,14},{7,15},{8,0},{9,1},... | collective-permute-start | bytes 442376 | tf_op jit(solution)/shard_map/ppermute | solution.py:198
  430.8 11.3 %collective-permute-start.39 = (f32[48,3072]{1,0:T(8,128)S(1)}, f32[48,3072]{1,0:T(8,128)S(1)}, u32[]{:S(2)}, u32[]{:S(2)}) collective-permute-start(f32[48,3072]{1,0:T(8,128)S(1)} %pad_maximum_fusion.12), channel_id=1, source_target_pairs={{0,2},{1,3},{2,0},{3,1},{4,6},{5,7},{6,4},{7,5},{8,10},{9,11},{10,... | collective-permute-start | bytes 1769480 | tf_op jit(solution)/shard_map/ppermute | solution.py:198
  439.6 16.6 %collective-permute-start.17 = (f32[192,768]{1,0:T(8,128)S(1)}, f32[192,768]{1,0:T(8,128)S(1)}, u32[]{:S(2)}, u32[]{:S(2)}) collective-permute-start(f32[192,768]{1,0:T(8,128)S(1)} %pad_maximum_fusion.10), channel_id=1, source_target_pairs={{0,2},{1,3},{2,0},{3,1},{4,6},{5,7},{6,4},{7,5},{8,10},{9,11},{10,... | collective-permute-start | bytes 1769480 | tf_op jit(solution)/shard_map/ppermute | solution.py:198
  442.4 25.5 %collective-permute-start.40 = (f32[96,3072]{1,0:T(8,128)S(1)}, f32[96,3072]{1,0:T(8,128)S(1)}, u32[]{:S(2)}, u32[]{:S(2)}) collective-permute-start(f32[96,3072]{1,0:T(8,128)S(1)} %pad_maximum_fusion.6), channel_id=1, source_target_pairs={{0,1},{1,0},{2,3},{3,2},{4,5},{5,4},{6,7},{7,6},{8,9},{9,8},{10,11... | collective-permute-start | bytes 3538952 | tf_op jit(solution)/shard_map/ppermute | solution.py:198
  443.1 50.3 %collective-permute-start.41 = (f32[96,3072]{1,0:T(8,128)S(1)}, f32[96,3072]{1,0:T(8,128)S(1)}, u32[]{:S(2)}, u32[]{:S(2)}) collective-permute-start(f32[96,3072]{1,0:T(8,128)S(1)} %pad_maximum_fusion.6), channel_id=1, source_target_pairs={{0,16},{16,0},{1,17},{17,1},{2,18},{18,2},{3,19},{19,3},{4,20},{20... | collective-permute-start | bytes 3538952 | tf_op jit(solution)/shard_map/ppermute | solution.py:201
  443.4 71.0 %collective-permute-start.73 = (f32[384,768]{1,0:T(8,128)S(1)}, f32[384,768]{1,0:T(8,128)S(1)}, u32[]{:S(2)}, u32[]{:S(2)}) collective-permute-start(f32[384,768]{1,0:T(8,128)S(1)} %pad_maximum_fusion.9), channel_id=1, source_target_pairs={{0,1},{1,0},{2,3},{3,2},{4,5},{5,4},{6,7},{7,6},{8,9},{9,8},{10,11... | collective-permute-start | bytes 3538952 | tf_op jit(solution)/shard_map/ppermute | solution.py:198
  449.1 44.1 %collective-permute-start.62 = (f32[384,768]{1,0:T(8,128)S(1)}, f32[384,768]{1,0:T(8,128)S(1)}, u32[]{:S(2)}, u32[]{:S(2)}) collective-permute-start(f32[384,768]{1,0:T(8,128)S(1)} %pad_maximum_fusion.8), channel_id=1, source_target_pairs={{0,1},{1,0},{2,3},{3,2},{4,5},{5,4},{6,7},{7,6},{8,9},{9,8},{10,11... | collective-permute-start | bytes 3538952 | tf_op jit(solution)/shard_map/ppermute | solution.py:198
  456.2 16.3 %collective-permute-start.28 = (f32[192,768]{1,0:T(8,128)S(1)}, f32[192,768]{1,0:T(8,128)S(1)}, u32[]{:S(2)}, u32[]{:S(2)}) collective-permute-start(f32[192,768]{1,0:T(8,128)S(1)} %pad_maximum_fusion.11), channel_id=1, source_target_pairs={{0,2},{1,3},{2,0},{3,1},{4,6},{5,7},{6,4},{7,5},{8,10},{9,11},{10,... | collective-permute-start | bytes 1769480 | tf_op jit(solution)/shard_map/ppermute | solution.py:198
  467.9 27.2 %collective-permute-start.42 = (f32[96,3072]{1,0:T(8,128)S(1)}, f32[96,3072]{1,0:T(8,128)S(1)}, u32[]{:S(2)}, u32[]{:S(2)}) collective-permute-start(f32[96,3072]{1,0:T(8,128)S(1)} %collective-permute-done.40), channel_id=1, source_target_pairs={{0,16},{16,0},{1,17},{17,1},{2,18},{18,2},{3,19},{19,3},{4,20},{20... | collective-permute-start | bytes 3538952 | tf_op jit(solution)/shard_map/ppermute | solution.py:201
  472.5 46.7 %collective-permute-start.74 = (f32[384,768]{1,0:T(8,128)S(1)}, f32[384,768]{1,0:T(8,128)S(1)}, u32[]{:S(2)}, u32[]{:S(2)}) collective-permute-start(f32[384,768]{1,0:T(8,128)S(1)} %pad_maximum_fusion.9), channel_id=1, source_target_pairs={{0,16},{16,0},{1,17},{17,1},{2,18},{18,2},{3,19},{19,3},{4,20},{20... | collective-permute-start | bytes 3538952 | tf_op jit(solution)/shard_map/ppermute | solution.py:201
  493.4 16.2 %collective-permute-start.51 = (f32[96,3072]{1,0:T(8,128)S(1)}, f32[96,3072]{1,0:T(8,128)S(1)}, u32[]{:S(2)}, u32[]{:S(2)}) collective-permute-start(f32[96,3072]{1,0:T(8,128)S(1)} %pad_maximum_fusion.7), channel_id=1, source_target_pairs={{0,1},{1,0},{2,3},{3,2},{4,5},{5,4},{6,7},{7,6},{8,9},{9,8},{10,11... | collective-permute-start | bytes 3538952 | tf_op jit(solution)/shard_map/ppermute | solution.py:198
  495.1 16.2 %collective-permute-start.64 = (f32[384,768]{1,0:T(8,128)S(1)}, f32[384,768]{1,0:T(8,128)S(1)}, u32[]{:S(2)}, u32[]{:S(2)}) collective-permute-start(f32[384,768]{1,0:T(8,128)S(1)} %collective-permute-done.62), channel_id=1, source_target_pairs={{0,16},{16,0},{1,17},{17,1},{2,18},{18,2},{3,19},{19,3},{4,20},{20... | collective-permute-start | bytes 3538952 | tf_op jit(solution)/shard_map/ppermute | solution.py:201
  496.0 18.9 %collective-permute-start.52 = (f32[96,3072]{1,0:T(8,128)S(1)}, f32[96,3072]{1,0:T(8,128)S(1)}, u32[]{:S(2)}, u32[]{:S(2)}) collective-permute-start(f32[96,3072]{1,0:T(8,128)S(1)} %pad_maximum_fusion.7), channel_id=1, source_target_pairs={{0,16},{16,0},{1,17},{17,1},{2,18},{18,2},{3,19},{19,3},{4,20},{20... | collective-permute-start | bytes 3538952 | tf_op jit(solution)/shard_map/ppermute | solution.py:201
  509.6 16.2 %collective-permute-start.19 = (f32[384,768]{1,0:T(8,128)S(1)}, f32[384,768]{1,0:T(8,128)S(1)}, u32[]{:S(2)}, u32[]{:S(2)}) collective-permute-start(f32[384,768]{1,0:T(8,128)S(1)} %pad_maximum_fusion.4), channel_id=1, source_target_pairs={{0,1},{1,0},{2,3},{3,2},{4,5},{5,4},{6,7},{7,6},{8,9},{9,8},{10,11... | collective-permute-start | bytes 3538952 | tf_op jit(solution)/shard_map/ppermute | solution.py:198
  514.3 28.6 %collective-permute-start.18 = (f32[384,768]{1,0:T(8,128)S(1)}, f32[384,768]{1,0:T(8,128)S(1)}, u32[]{:S(2)}, u32[]{:S(2)}) collective-permute-start(f32[384,768]{1,0:T(8,128)S(1)} %pad_maximum_fusion.4), channel_id=1, source_target_pairs={{0,16},{16,0},{1,17},{17,1},{2,18},{18,2},{3,19},{19,3},{4,20},{20... | collective-permute-start | bytes 3538952 | tf_op jit(solution)/shard_map/ppermute | solution.py:201
  514.9 23.6 %collective-permute-start.29 = (f32[384,768]{1,0:T(8,128)S(1)}, f32[384,768]{1,0:T(8,128)S(1)}, u32[]{:S(2)}, u32[]{:S(2)}) collective-permute-start(f32[384,768]{1,0:T(8,128)S(1)} %pad_maximum_fusion.5), channel_id=1, source_target_pairs={{0,1},{1,0},{2,3},{3,2},{4,5},{5,4},{6,7},{7,6},{8,9},{9,8},{10,11... | collective-permute-start | bytes 3538952 | tf_op jit(solution)/shard_map/ppermute | solution.py:198
  515.2 23.3 %collective-permute-start.75 = (f32[384,768]{1,0:T(8,128)S(1)}, f32[384,768]{1,0:T(8,128)S(1)}, u32[]{:S(2)}, u32[]{:S(2)}) collective-permute-start(f32[384,768]{1,0:T(8,128)S(1)} %collective-permute-done.73), channel_id=1, source_target_pairs={{0,16},{16,0},{1,17},{17,1},{2,18},{18,2},{3,19},{19,3},{4,20},{20... | collective-permute-start | bytes 3538952 | tf_op jit(solution)/shard_map/ppermute | solution.py:201
  519.2 28.2 %collective-permute-start.30 = (f32[384,768]{1,0:T(8,128)S(1)}, f32[384,768]{1,0:T(8,128)S(1)}, u32[]{:S(2)}, u32[]{:S(2)}) collective-permute-start(f32[384,768]{1,0:T(8,128)S(1)} %pad_maximum_fusion.5), channel_id=1, source_target_pairs={{0,16},{16,0},{1,17},{17,1},{2,18},{18,2},{3,19},{19,3},{4,20},{20... | collective-permute-start | bytes 3538952 | tf_op jit(solution)/shard_map/ppermute | solution.py:201
  525.8 17.1 %collective-permute-start.20 = (f32[384,768]{1,0:T(8,128)S(1)}, f32[384,768]{1,0:T(8,128)S(1)}, u32[]{:S(2)}, u32[]{:S(2)}) collective-permute-start(f32[384,768]{1,0:T(8,128)S(1)} %collective-permute-done.19), channel_id=1, source_target_pairs={{0,16},{16,0},{1,17},{17,1},{2,18},{18,2},{3,19},{19,3},{4,20},{20... | collective-permute-start | bytes 3538952 | tf_op jit(solution)/shard_map/ppermute | solution.py:201
  538.5 9.0 %collective-permute-start.31 = (f32[384,768]{1,0:T(8,128)S(1)}, f32[384,768]{1,0:T(8,128)S(1)}, u32[]{:S(2)}, u32[]{:S(2)}) collective-permute-start(f32[384,768]{1,0:T(8,128)S(1)} %collective-permute-done.29), channel_id=1, source_target_pairs={{0,16},{16,0},{1,17},{17,1},{2,18},{18,2},{3,19},{19,3},{4,20},{20... | collective-permute-start | bytes 3538952 | tf_op jit(solution)/shard_map/ppermute | solution.py:201
  (82 other events, 374.7 us)

commit v2 on v1

v2 whole, which is shorter than its diff:
```python
import jax
import jax.numpy as jnp
from jax import lax
from jax.experimental import pallas as pl
from jax.experimental.pallas import tpu as pltpu
from jax.sharding import PartitionSpec as P

F32 = jnp.float32
BF16 = jnp.bfloat16
LANES = 128


def cost(micros):
    return pl.CostEstimate(flops=0, bytes_accessed=int(micros * 3.4e6), transcendentals=0)


def col_spec(rows):
    return pl.BlockSpec((rows, LANES), lambda g: (0, g))


def per_group(kernel, ins, outs, scratch, micros):
    width = ins[0].shape[1]
    return pl.pallas_call(
        kernel,
        grid=(width // LANES,),
        in_specs=[col_spec(x.shape[0]) for x in ins],
        out_specs=[col_spec(rows) for rows, _ in outs],
        out_shape=[jax.ShapeDtypeStruct((rows, width), kind) for rows, kind in outs],
        scratch_shapes=scratch,
        cost_estimate=cost(micros),
        compiler_params=pltpu.CompilerParams(vmem_limit_bytes=32 * 1024 * 1024),
    )(*ins)


def folded(product):
    return jnp.sum(product.reshape(product.shape[0] // 8, 8, product.shape[1]), 0)


def unfold(parts_ref, rows):
    total = parts_ref[pl.ds(0, rows, stride=8), :]
    for s in range(1, 8):
        total = total + parts_ref[pl.ds(s, rows, stride=8), :]
    return total


def both_kernel(own_ref, far_ref, out_ref):
    rows = own_ref.shape[0]
    out_ref[0:rows, :] = own_ref[...]
    out_ref[rows:, :] = far_ref[...].astype(BF16)


def both(own, far):
    rows, width = own.shape
    block = 3 * LANES
    return pl.pallas_call(
        both_kernel,
        grid=(width // block,),
        in_specs=[pl.BlockSpec((rows, block), lambda g: (0, g))] * 2,
        out_specs=pl.BlockSpec((2 * rows, block), lambda g: (0, g)),
        out_shape=jax.ShapeDtypeStruct((2 * rows, width), BF16),
        cost_estimate=cost(rows * width * 10 / 3.4e6),
    )(own, far)


def ends_kernel(key_ref, value_ref, rim_ref, taps_ref, rate_ref, shifted_ref, inputs_ref, end_ref, pad):
    rows = key_ref.shape[0]
    pad[0:8, :] = rim_ref[...]
    pad[8:, :] = key_ref[...]
    shifted = taps_ref[0:1, :] * pad[8:, :]
    for j in range(1, 4):
        shifted = shifted + taps_ref[j : j + 1, :] * pad[8 - j : 8 - j + rows, :]
    shifted_ref[...] = shifted
    inputs_ref[...] = shifted * value_ref[...]
    decay = jnp.exp(-rate_ref[...])

    def lap(i, state):
        for k in range(16):
            state = decay * state + inputs_ref[pl.ds(i * 16 + k, 1), :]
        return state

    end_ref[...] = lax.fori_loop(0, rows // 16, lap, jnp.zeros_like(decay))


def mix_kernel(
    inputs_ref, query_ref, enter_ref, rate_ref, read_ref, skip_ref, mixed_ref, gated_ref, parts
):
    rows = inputs_ref.shape[0]
    decay = jnp.exp(-rate_ref[...])
    read = read_ref[...]

    def lap(i, state):
        for k in range(16):
            t = i * 16 + k
            state = decay * state + inputs_ref[pl.ds(t, 1), :]
            parts[pl.ds(pl.multiple_of(t * 8, 8), 8), :] = folded(read * state)
        return state

    lax.fori_loop(0, rows // 16, lap, enter_ref[...])
    mixed = unfold(parts, rows) + skip_ref[...] * inputs_ref[...]
    mixed_ref[...] = mixed
    gated_ref[...] = (query_ref[...] * mixed).astype(BF16)


def towards_kernel(
    grad_ref, query_ref, mixed_ref, rate_ref, grad_query_ref, grad_mixed_ref, start_ref
):
    rows = grad_ref.shape[0]
    grad_query_ref[...] = (grad_ref[...] * mixed_ref[...]).astype(BF16)
    grad_mixed_ref[...] = grad_ref[...] * query_ref[...]
    decay = jnp.exp(-rate_ref[...])

    def lap(i, state):
        for k in range(16):
            state = decay * state + grad_mixed_ref[pl.ds(rows - 1 - i * 16 - k, 1), :]
        return state

    start_ref[...] = lax.fori_loop(0, rows // 16, lap, jnp.zeros_like(decay))


def back_kernel(
    grad_ref,
    inputs_ref,
    shifted_ref,
    value_ref,
    key_ref,
    rim_ref,
    taps_ref,
    rate_ref,
    read_ref,
    skip_ref,
    enter_ref,
    adjoint_ref,
    grad_value_ref,
    grad_key_ref,
    head_ref,
    sum_ref,
    slope_ref,
    small_ref,
    parts,
    pad,
):
    rows = grad_ref.shape[0]
    decay = jnp.exp(-rate_ref[...])
    read = read_ref[...]
    zero = jnp.zeros_like(decay)

    def lap(i, carry):
        adjoint, ramp, total, slope = carry
        for k in range(8):
            t = rows - 1 - i * 8 - k
            entry = inputs_ref[pl.ds(t, 1), :]
            slope = slope + entry * ramp
            adjoint = decay * adjoint + grad_ref[pl.ds(t, 1), :]
            total = total + entry * adjoint
            parts[pl.ds(pl.multiple_of(t * 8, 8), 8), :] = folded(read * adjoint)
            ramp = decay * ramp + adjoint
        return adjoint, ramp, total, slope

    _, ramp, total, slope = lax.fori_loop(
        0, rows // 8, lap, (adjoint_ref[...], zero, zero, zero)
    )
    sum_ref[...] = total
    slope_ref[...] = slope + enter_ref[...] * ramp
    grad = grad_ref[...]
    grad_inputs = unfold(parts, rows) + skip_ref[...] * grad
    grad_value_ref[...] = (grad_inputs * shifted_ref[...]).astype(BF16)
    grad_shifted = grad_inputs * value_ref[...]
    pad[0:rows, :] = grad_shifted
    pad[rows:, :] = jnp.zeros_like(head_ref)
    head_ref[...] = pad[0:8, :]
    grad_key = taps_ref[0:1, :] * grad_shifted
    for j in range(1, 4):
        grad_key = grad_key + taps_ref[j : j + 1, :] * pad[j : j + rows, :]
    grad_key_ref[...] = grad_key
    pad[0:8, :] = rim_ref[...]
    pad[8:, :] = key_ref[...]
    small = [
        jnp.sum(grad_shifted * pad[8 - j : 8 - j + rows, :], 0, keepdims=True) for j in range(4)
    ]
    small.append(jnp.sum(grad * inputs_ref[...], 0, keepdims=True))
    small.append(jnp.zeros((3, LANES), F32))
    small_ref[...] = jnp.concatenate(small, 0)


def bits_of(count):
    out, step = [], 1
    while step < count:
        out.append(step)
        step *= 2
    return out


class Wires:
    def __init__(self):
        self.batch, self.seq = lax.axis_size("batch"), lax.axis_size("seq")
        bits = bits_of(self.seq)
        swapped = bits[1::-1] + bits[2:]
        self.orders = (tuple(bits), tuple(swapped))
        self.stages = [(k,) for k in range(len(bits))]
        self.spare = bits_of(self.batch)[1:]
        self.core = lax.axis_index("batch") % 2
        self.place = lax.axis_index("seq")

    def spot(self, stage, core=None):
        core = self.core if core is None else core
        numbers = []
        for order in self.orders:
            digits = [(self.place // order[k]) % 2 for k in self.stages[stage]]
            numbers.append(sum(d * 2**i for i, d in enumerate(digits)))
        return jnp.where(core == 0, *numbers)

    def swap(self, value, stage, flip=1):
        pairs = []
        for b in range(self.batch):
            order = self.orders[b % 2]
            step = sum(order[k] for i, k in enumerate(self.stages[stage]) if flip // 2**i % 2)
            pairs += [(b * self.seq + s, b * self.seq + (s ^ step)) for s in range(self.seq)]
        return lax.ppermute(value, ("batch", "seq"), pairs)

    def swap_batch(self, value, step):
        return lax.ppermute(value, "batch", [(b, b ^ step) for b in range(self.batch)])

    def other_core(self, value):
        return self.swap_batch(value.astype(F32), 1)

    def joined(self, pieces, shape, kind, tail=0):
        rows, width = pieces[0].shape
        main = rows - tail
        here, there = self.spot(0), self.spot(0, 1 - self.core)
        places = jnp.stack([self.core, here, here ^ 1, there, there ^ 1]).astype(jnp.int32)
        outs = [jax.ShapeDtypeStruct(shape, F32)] * (2 if kind == "tensors" else 1)
        if tail:
            outs = outs + [jax.ShapeDtypeStruct((4 * tail, width), F32)]

        def kernel(places_ref, *refs):
            sources, targets, (buffer, sems_in, sems_out) = refs[:4], refs[4:-3], refs[-3:]
            reads = [
                pltpu.make_async_copy(sources[k], buffer.at[k], sems_in.at[k]) for k in range(4)
            ]
            for read in reads:
                read.start()
            core = places_ref[0]
            for k in range(4):
                reads[k].wait()
                owner = core if k < 2 else 1 - core
                spot = places_ref[1 + k]
                block = buffer.at[k, pl.ds(0, main)]

                def send(target, k=k, block=block):
                    pltpu.make_async_copy(block, target, sems_out.at[k]).start()

                if kind == "tensors":
                    for which in range(2):
                        window = targets[which].at[pl.ds(pl.multiple_of(spot * main, 8), main)]
                        pl.when(owner == which)(lambda window=window, send=send: send(window))
                elif kind == "rows":
                    place = pl.multiple_of((2 * owner + spot) * main, 8)
                    send(targets[0].at[pl.ds(place, main)])
                else:
                    place = pl.multiple_of(spot * main, 8)
                    column = pl.multiple_of(owner * width, LANES)
                    send(targets[0].at[pl.ds(place, main), pl.ds(column, width)])
                if tail:
                    place = pl.multiple_of((2 * owner + spot) * tail, 8)
                    pltpu.make_async_copy(
                        buffer.at[k, pl.ds(main, tail)],
                        targets[-1].at[pl.ds(place, tail)],
                        sems_out.at[4 + k],
                    ).start()
            for k in range(4):
                window = targets[0].at[pl.ds(0, main), pl.ds(0, width)]
                pltpu.make_async_copy(buffer.at[k, pl.ds(0, main)], window, sems_out.at[k]).wait()
                if tail:
                    pltpu.make_async_copy(
                        buffer.at[k, pl.ds(main, tail)],
                        targets[-1].at[pl.ds(0, tail)],
                        sems_out.at[4 + k],
                    ).wait()

        moved = 4 * rows * width * 4
        return pl.pallas_call(
            kernel,
            in_specs=[pl.BlockSpec(memory_space=pltpu.SMEM)]
            + [pl.BlockSpec(memory_space=pl.ANY)] * 4,
            out_specs=[pl.BlockSpec(memory_space=pl.ANY)] * len(outs),
            out_shape=outs,
            scratch_shapes=[
                pltpu.VMEM((4, rows, width), F32),
                pltpu.SemaphoreType.DMA((4,)),
                pltpu.SemaphoreType.DMA((8,)),
            ],
            cost_estimate=cost(2 * moved / 3.4e6),
            compiler_params=pltpu.CompilerParams(vmem_limit_bytes=moved + 4 * 1024 * 1024),
        )(places, *pieces)


def part(value, which, count, axis=0):
    size = value.shape[axis] // count
    return lax.dynamic_slice_in_dim(value, which * size, size, axis)


class Turns:
    def __init__(self, strict):
        self.strict, self.made = strict, None

    def take(self, value):
        if not self.strict or self.made is None:
            return value
        return lax.optimization_barrier((value, self.made))[0]

    def give(self, made):
        self.made = made


class Sum:
    def __init__(self, wires, turns, left, right, tail=None):
        self.wires, self.turns = wires, turns
        self.left, self.right, self.tail = left, right, tail
        self.count = len(wires.stages)

    def step(self, number):
        if number == 0:
            self.begin()
        elif number < self.count:
            self.scatter(number)
        else:
            self.gather(2 * self.count - 1 - number)

    def begin(self):
        wires, turns = self.wires, self.turns
        spot = wires.spot(0)
        left = turns.take(self.left)

        def piece(which):
            made = weight_grad(part(left, which, 2, 1), self.right)
            if self.tail is not None:
                made = jnp.concatenate([made, sum(part(x, which, 2) for x in self.tail)], 0)
            return made

        send = piece(1 - spot)
        arriving = wires.swap(send, 0)
        keep = piece(spot)
        turns.give((send, keep))
        self.terms = [keep, arriving]

    def scatter(self, stage):
        wires, turns = self.wires, self.turns
        ways = 2 ** len(wires.stages[stage])
        spot = wires.spot(stage)
        terms = self.terms[:-1] + [turns.take(self.terms[-1])]
        sends = [sum(part(t, spot ^ flip, ways) for t in terms) for flip in range(1, ways)]
        turns.give(sends)
        arriving = [wires.swap(send, stage, flip + 1) for flip, send in enumerate(sends)]
        self.terms = [sum(part(t, spot, ways) for t in terms)] + arriving

    def gather(self, stage):
        wires, turns = self.wires, self.turns
        if stage == self.count - 1:
            block = sum(self.terms[:-1]) + turns.take(self.terms[-1])
            for step in wires.spare:
                block = block + wires.swap_batch(block, step)
        else:
            ways = 2 ** len(wires.stages[stage + 1])
            spot = wires.spot(stage + 1)
            pieces = self.pieces[:-1] + [turns.take(self.pieces[-1])]
            rows = []
            for where in range(ways):
                picked = pieces[0]
                for flip in range(1, ways):
                    picked = jnp.where(spot == where ^ flip, pieces[flip], picked)
                rows.append(picked)
            block = jnp.concatenate(rows, 0)
        turns.give(block)
        ways = 2 ** len(wires.stages[stage])
        self.pieces = [block] + [wires.swap(block, stage, flip) for flip in range(1, ways)]
        if stage == 0:
            self.far = wires.swap_batch(block, 1)

    def cross(self):
        self.pieces[1] = self.turns.take(self.pieces[1])
        self.turns.give(self.pieces[1])
        self.far_other = self.wires.swap_batch(self.pieces[1], 1)

    def join(self, shape, kind, tail=0):
        pieces = (*self.pieces, self.far, self.turns.take(self.far_other))
        whole = self.wires.joined(pieces, shape, kind, tail)
        self.turns.give(whole[0])
        return whole


ORDER = (
    "X", "A00", "G1", "G2", "K1", "P", "A10", "P", "A01", "P",
    "A02", "A20", "B0", "A12", "A30", "A11", "A22", "R", "A40", "E",
    "A21", "A03", "A50", "A32", "A42", "A13", "A31", "A52", "A60", "A23",
    "A41", "A62", "A70", "A33", "A51", "A61", "F0", "A43", "A72", "A53",
    "A71", "F2", "J0", "A63", "A73", "F1", "J2", "J1", "F3", "J3",
)


def plain_order(sums, stages):
    names = ["X", "G1", "G2", "K1", "B0", "R", "E"]
    kinds = [f"A{k}" for k in range(2 * stages)] + ["F", "J"]
    return names + [f"{kind}{c}" for kind in kinds for c in range(sums)]


class Prefix:
    def __init__(self, turns, ends, rate, rows, backward):
        self.turns, self.rate, self.rows = turns, rate, rows
        self.count = lax.axis_size("seq")
        place = lax.axis_index("seq")
        self.rank = self.count - 1 - place if backward else place
        self.bits = bits_of(self.count)
        self.total, self.entering = ends, jnp.zeros_like(ends)
        self.done = 0
        self.start()

    def start(self):
        step = self.bits[self.done]
        pairs = [(s, s ^ step) for s in range(self.count)]
        self.arriving = lax.ppermute(self.total, "seq", pairs)

    def step(self):
        step = self.bits[self.done]
        arriving = self.turns.take(self.arriving)
        upper = (self.rank // step) % 2 == 1
        behind = ((self.rank % step) * self.rows).astype(F32)
        decayed = jnp.exp(-self.rate * behind) * arriving
        self.entering = jnp.where(upper, self.entering + decayed, self.entering)
        self.done += 1
        if self.done < len(self.bits):
            early = jnp.where(upper, arriving, self.total)
            late = jnp.where(upper, self.total, arriving)
            self.total = jnp.exp(-self.rate * (step * self.rows)) * early + late
            self.turns.give(self.total)
            self.start()

    def finish(self):
        while self.done < len(self.bits):
            self.step()
        return self.entering


def layer_norm(rows_in, gain):
    centred = rows_in - jnp.mean(rows_in, -1, keepdims=True)
    spread = jnp.mean(centred * centred, -1, keepdims=True)
    return centred * lax.rsqrt(spread + 1e-05) * gain


def gelu_tanh(upper):
    return jax.nn.gelu(upper, approximate=True)


def product(left, right):
    return jnp.dot(left, right, preferred_element_type=F32)


def weight_grad(left, right):
    return jnp.einsum("ti,tj->ij", left, right, preferred_element_type=F32)


def back_product(grad_rows, weight):
    return jnp.einsum("tj,ij->ti", grad_rows, weight, preferred_element_type=F32)


def local(
    tokens,
    w_query,
    w_key,
    w_value,
    w_out,
    w_up,
    w_down,
    gain_mix,
    gain_ffn,
    taps,
    rate,
    gain_b,
    gain_c,
    skip,
    cotangent,
):
    _, rows, width = tokens.shape
    count = lax.axis_size("seq")
    states = rate.shape[0]
    wires = Wires()
    skip_row = skip.reshape(1, width)
    scale = gain_b * jnp.sqrt(-jnp.expm1(-2.0 * rate))
    read = gain_c * scale

    flat_in = tokens.astype(F32).reshape(rows, width)
    normed, norm_pull = jax.vjp(layer_norm, flat_in, gain_mix)
    mixed_in = normed.astype(BF16)
    grad_out = cotangent.reshape(rows, width)
    all_grad_out = both(grad_out, wires.other_core(grad_out))
    all_mixed_in = both(mixed_in, wires.other_core(mixed_in))
    rim_own = product(layer_norm(flat_in[rows - 8 :], gain_mix).astype(BF16), w_key)
    rim = lax.ppermute(rim_own, "seq", [(s, s + 1) for s in range(count - 1)])
    queries = product(mixed_in, w_query)
    key_rows = product(mixed_in, w_key)
    values = product(mixed_in, w_value)
    share = rows * states * width / (256 * 64 * 768)
    shifted, inputs, ends = per_group(
        ends_kernel,
        (key_rows, values, rim, taps, rate),
        ((rows, F32), (rows, F32), (states, F32)),
        [pltpu.VMEM((rows + 8, LANES), F32)],
        4.3 * share,
    )
    entering = Prefix(Turns(False), ends, rate, rows, False).finish()
    mixed, gated = per_group(
        mix_kernel,
        (inputs, queries, entering, rate, read, skip_row),
        ((rows, F32), (rows, BF16)),
        [pltpu.VMEM((rows * 8, LANES), F32)],
        8.2 * share,
    )
    hidden = flat_in + product(gated, w_out)
    ffn_normed, ffn_pull = jax.vjp(layer_norm, hidden, gain_ffn)
    ffn_in = ffn_normed.astype(BF16)
    upper = product(ffn_in, w_up)
    activated, gelu_pull = jax.vjp(gelu_tanh, upper)
    act = activated.astype(BF16)

    strict = len(wires.stages) == 4
    turns = Turns(strict)
    sums, made, whole = {}, {}, {}
    first = wires.core == 0

    def own(value, axis=1):
        return part(value, wires.core, 2, axis)

    def others(value, axis=1):
        return part(value, 1 - wires.core, 2, axis)

    def forward_over():
        all_act = both(own(act), wires.other_core(others(act)))
        sums[0] = Sum(wires, turns, all_act, all_grad_out)
        made["ffn_in"] = both(ffn_in, wires.other_core(ffn_in))

    def up_back():
        grad_act = back_product(turns.take(grad_out), w_down)
        grad_upper = gelu_pull(grad_act)[0].astype(BF16)
        made["grad_upper"] = grad_upper
        turns.give(grad_upper)
        right = both(own(grad_upper), wires.other_core(others(grad_upper)))
        sums[1] = Sum(wires, turns, made["ffn_in"], right)

    def branch_back():
        grad_ffn = back_product(turns.take(made["grad_upper"]), w_up)
        grad_hidden_norm, made["d_gain_ffn"] = ffn_pull(grad_ffn)
        made["grad_hidden"] = grad_out.astype(F32) + grad_hidden_norm
        made["grad_branch"] = made["grad_hidden"].astype(BF16)
        made["grad_gated"] = back_product(made["grad_branch"], w_out)
        turns.give(made["grad_gated"])

    def towards():
        made["grad_queries"], made["grad_mixed"], starts = per_group(
            towards_kernel,
            (turns.take(made["grad_gated"]), queries, mixed, rate),
            ((rows, BF16), (rows, F32), (states, F32)),
            [],
            4.8 * share,
        )
        turns.give(starts)
        all_gated = both(gated, wires.other_core(gated))
        sent = jnp.where(first, made["grad_queries"], made["grad_branch"])
        kept = jnp.where(first, made["grad_branch"], made["grad_queries"])
        left = jnp.where(first, all_gated, all_mixed_in)
        sums[2] = Sum(wires, turns, left, both(kept, wires.other_core(sent)))
        made["prefix"] = Prefix(turns, starts, rate, rows, True)

    def mixer_back():
        adjoint = turns.take(made["prefix"].finish())
        out = per_group(
            back_kernel,
            (
                made["grad_mixed"],
                inputs,
                shifted,
                values,
                key_rows,
                rim,
                taps,
                rate,
                read,
                skip_row,
                entering,
                adjoint,
            ),
            ((rows, BF16), (rows, F32), (8, F32), (states, F32), (states, F32), (8, F32)),
            [pltpu.VMEM((rows * 8, LANES), F32), pltpu.VMEM((rows + 8, LANES), F32)],
            23 * share,
        )
        made["grad_values"], made["grad_keys"], head, *made["small"] = out
        turns.give(head)
        made["behind"] = lax.ppermute(head, "seq", [(s + 1, s) for s in range(count - 1)])

    def rim_back():
        behind, local_keys = turns.take(made["behind"]), made["grad_keys"]
        padded = jnp.concatenate([jnp.zeros_like(behind), behind[:4]], 0)
        late = sum(taps[j] * padded[j : j + 8] for j in range(1, 4))
        made["grad_keys"] = jnp.concatenate(
            [local_keys[: rows - 8], local_keys[rows - 8 :] + late], 0
        ).astype(BF16)
        turns.give(made["grad_keys"])
        sent = jnp.where(first, made["grad_values"], made["grad_keys"])
        kept = jnp.where(first, made["grad_keys"], made["grad_values"])
        made["both"] = both(kept, wires.other_core(sent))

    def input_back():
        grad_normed = (
            back_product(turns.take(made["grad_keys"]), w_key)
            + back_product(made["grad_queries"], w_query)
            + back_product(made["grad_values"], w_value)
        )
        grad_input_norm, made["d_gain_mix"] = norm_pull(grad_normed)
        made["d_tokens"] = (made["grad_hidden"] + grad_input_norm).astype(BF16)
        turns.give(made["d_tokens"])

        totals, slopes, small = made["small"]
        gains = jnp.stack([made["d_gain_mix"], made["d_gain_ffn"]])
        part_a = jnp.concatenate([totals, small[:5], jnp.zeros((extra - states - 5, width), F32)], 0)
        part_b = jnp.concatenate([slopes, gains, jnp.zeros((extra - states - 2, width), F32)], 0)
        tail = (
            jnp.where(first, part_a, part_b),
            wires.swap_batch(jnp.where(first, part_b, part_a), 1),
        )
        sums[3] = Sum(wires, turns, all_mixed_in, made["both"], tail)

    extra = 2 * 64 * (-(-(states + 5) // 128))
    joins = (
        (w_down.shape, "rows"),
        (w_up.shape, "columns"),
        (w_out.shape, "tensors"),
        (w_key.shape, "tensors", extra // 2),
    )
    steps = {
        "X": forward_over,
        "G1": up_back,
        "G2": branch_back,
        "K1": towards,
        "P": lambda: made["prefix"].step(),
        "B0": mixer_back,
        "R": rim_back,
        "E": input_back,
    }
    for name in ORDER if strict and ORDER else plain_order(4, len(wires.stages)):
        with jax.named_scope(name):
            if name[0] == "A":
                sums[int(name[-1])].step(int(name[1:-1]))
            elif name[0] == "F":
                sums[int(name[-1])].cross()
            elif name[0] == "J":
                whole[int(name[-1])] = sums[int(name[-1])].join(*joins[int(name[-1])])
            else:
                steps[name]()
    output = hidden + product(act, w_down)
    d_down, d_up = whole[0][0], whole[1][0]
    d_out, d_query = whole[2]
    d_key, d_value, tails = whole[3]
    part_a, part_b = tails[:extra], tails[extra:]
    d_tokens = made["d_tokens"].reshape(tokens.shape)
    totals, slopes = part_a[:states], part_b[:states]
    d_scale = gain_c * totals
    d_decay = read * slopes
    root = jnp.sqrt(-jnp.expm1(-2.0 * rate))
    d_rate = -jnp.exp(-rate) * d_decay + d_scale * gain_b * jnp.exp(-2.0 * rate) / root
    return (
        output.astype(BF16).reshape(tokens.shape),
        d_tokens,
        d_query,
        d_key,
        d_value,
        d_out,
        d_up,
        d_down,
        part_b[states],
        part_b[states + 1],
        part_a[states : states + 4],
        d_rate,
        d_scale * root,
        scale * totals,
        part_a[states + 4],
    )


def half_columns(value, which):
    columns = value.shape[1] // 2
    return lax.dynamic_slice_in_dim(value, which * columns, columns, 1)


def solution(mesh):
    split = P("batch", "seq", None)
    in_specs = (split,) + (P(),) * 13 + (split,)
    out_specs = (split, split) + (P(),) * 13
    return jax.shard_map(local, mesh=mesh, in_specs=in_specs, out_specs=out_specs, check_vma=False)
```

time: 564 us -> 445 us (0.79); the launches traced: 554 us -> 443 us
  waiting for transfers between devices: 348 us -> 178 us
  Pallas kernels: 40.2 us -> 82 us
  other arithmetic: 42.6 us -> 69 us
  starting transfers between devices: 77.2 us -> 60.7 us
  matrix products: 25.9 us -> 35.3 us
    ppermute x56 -> x32, waiting for transfers between devices: 309 us -> 136 us  [swap(): return lax.ppermute(value, ('batch', 'seq'), pairs)]
    pallas_call x0 -> x12, Pallas kernels: none -> 42.5 us  [the longest x4 22.4 us: joined(): pl.pallas_call(kernel, in_specs=[pl.BlockSpec(memory_space=pltpu.SMEM)] +...]
    add x40 -> x22, other arithmetic: 11.2 us -> 31.4 us  [the longest x8 22 us: scatter(): self.terms = [sum((part(t, spot, ways) for t in terms))] + arriving]
    ppermute x56 -> x32, starting transfers between devices: 53.8 us -> 37.8 us  [swap(): return lax.ppermute(value, ('batch', 'seq'), pairs)]
    ppermute x21 -> x17, waiting for transfers between devices: 3.63 us -> 17.1 us  [swap_batch(): lax.ppermute(value, 'batch', [(b, b ^ step) for b in range(self.batch)])]
    unnamed x15 -> x2, other arithmetic: 11.5 us -> 0.01 us
    convert_element_type x2 -> x10, other arithmetic: 0.33 us -> 10.5 us  [the longest x7 8.31 us: other_core(): return self.swap_batch(value.astype(F32), 1)]
    ppermute x9, waiting for transfers between devices: 35.4 us -> 25.2 us  [the longest x8 25.2 us: start(): self.arriving = lax.ppermute(self.total, 'seq', pairs)]
  transfers between devices with their start and end apart: 87 -> 59, of which waited for: 51 -> 26; matrix products, arithmetic and copies ran while one was open for 8% -> 19% of each run, Pallas kernels for 0% -> 15%
where the time goes in v2:
time: 445 us; the launch traced here: 443 us
  waiting for transfers between devices  178 us (40%)
  Pallas kernels  82 us (18%)
  other arithmetic  69 us (16%)
  starting transfers between devices  60.7 us (14%)
  matrix products  35.3 us (8%)
  local copies, waits for them, and re-layouts  15.8 us (4%)
    ppermute x32, waiting for transfers between devices, swap(): return lax.ppermute(value, ('batch', 'seq'), pairs)  136 us
    pallas_call x4, Pallas kernels, per_group(): pl.pallas_call(kernel, grid=(width // LANES,), in_specs=[col_spec(x.shape...  39.5 us
    ppermute x32, starting transfers between devices, swap(): return lax.ppermute(value, ('batch', 'seq'), pairs)  37.8 us
    ppermute x8, waiting for transfers between devices, start(): self.arriving = lax.ppermute(self.total, 'seq', pairs)  25.2 us
    pallas_call x4, Pallas kernels, joined(): pl.pallas_call(kernel, in_specs=[pl.BlockSpec(memory_space=pltpu.SMEM)] +...  22.4 us
    add x8, other arithmetic, scatter(): self.terms = [sum((part(t, spot, ways) for t in terms))] + arriving  22 us
    pallas_call x8, Pallas kernels, both(): pl.pallas_call(both_kernel, grid=(width // block,), in_specs=[pl.BlockSpe...  20 us
    ppermute x17, waiting for transfers between devices, swap_batch(): lax.ppermute(value, 'batch', [(b, b ^ step) for b in range(self.batch)])  17.1 us
  transfers between devices with their start and end apart: 59, of which 26 were waited for; matrix products, arithmetic and copies ran while one was open for 19% of the time, Pallas kernels for 15%

profile of v2, /device:TPU:0, one launch (start us, length us, event | category | flops | bytes accessed | tf_op | source)
XLA Modules:
  0.0 443.0 jit_solution(12852346983052448510)
XLA Ops:
  3.2 4.8 %collective-permute-start = (f32[8,768]{1,0:T(8,128)S(1)}, f32[8,768]{1,0:T(8,128)S(1)}, u32[]{:S(2)}, u32[]{:S(2)}) collective-permute-start(f32[8,768]{1,0:T(8,128)S(1)} %fusion.50), channel_id=1, source_target_pairs={{0,1},{1,2},{2,3},{3,4},{4,5},{5,6},{6,7},{7,8},{8,9},{9,10},{10,1... | collective-permute-start | bytes 73736 | tf_op jit(solution)/shard_map/ppermute | solution.py:497
  11.9 4.2 shard_map.262
  19.5 5.0 %collective-permute-done.1 = f32[64,768]{1,0:T(8,128)} collective-permute-done((f32[64,768]{1,0:T(8,128)S(1)}, f32[64,768]{1,0:T(8,128)}, u32[]{:S(2)}, u32[]{:S(2)}) %collective-permute-start.1) | collective-permute-done | bytes 196640 | tf_op jit(solution)/shard_map/ppermute | solution.py:420
  24.4 1.9 fusion.34
  27.8 4.4 collective-permute-done.2
  36.1 3.6 collective-permute-done.3
  40.7 2.9 collective-permute-start.4
  45.6 3.9 collective-permute-done.4
  50.6 8.3 %shard_map.263 = (f32[256,768]{1,0:T(8,128)S(1)}, bf16[256,768]{1,0:T(8,128)(2,1)S(1)}) custom-call(f32[256,768]{1,0:T(8,128)S(1)} %copy-done.7, f32[256,768]{1,0:T(8,128)S(1)} %fusion.63.query_ref, f32[64,768]{1,0:T(8,128)S(1)} %add_select_fusion.3.enter_ref, f32[64,768]{1,0:T(8,128)S(1)} %copy-done.2, f32[64,768]{1,0:T(8,128)S(1)} %get-tuple-element.221.read_ref, ...), custom_call_target="tpu_custom_call" | custom-call | bytes 27880000 | tf_op jit(solution)/shard_map/pallas_call | solution.py:23
  62.3 3.6 multiply_convert_fusion
  69.4 3.4 collective-permute-done.6.far_ref
  72.8 2.1 shard_map.264
  76.4 3.8 X.2
  80.2 3.7 fusion.11
  83.9 2.2 fusion.9
  87.7 5.1 %fusion.6 = bf16[256,3072]{1,0:T(8,128)(2,1)S(1)} fusion(f32[256,3072]{1,0:T(8,128)S(1)} %copy-done.104, bf16[256,768]{1,0:T(8,128)(2,1)S(1)} %bitcast.73, bf16[3072,768]{1,0:T(8,128)(2,1)} %param.21), kind=kOutput, calls=%fused_computation.8 | convolution fusion | flops 1223688192 | bytes 9830400 | tf_op jit(solution)/shard_map/G1/tj,ij->ti/dot_general | solution.py:462
  92.9 2.2 multiply_reduce_fusion
  99.3 4.2 K1.3
  106.8 2.1 shard_map.265
  108.9 2.1 K1.4
  111.0 8.4 %collective-permute-done.7 = f32[64,768]{1,0:T(8,128)S(1)} collective-permute-done((f32[64,768]{1,0:T(8,128)S(1)}, f32[64,768]{1,0:T(8,128)S(1)}, u32[]{:S(2)}, u32[]{:S(2)}) %collective-permute-start.7) | collective-permute-done | bytes 196640 | tf_op jit(solution)/shard_map/K1/ppermute | solution.py:420
  121.7 2.1 broadcast_select_fusion
  123.8 2.1 X.3
  125.9 2.1 K1.5
  128.0 3.8 G1.1
  131.8 4.2 dynamic-slice_add_fusion.2
  138.4 2.2 fusion.27
  142.0 2.2 fusion.25
  148.3 2.2 collective-permute-start.13
  150.5 2.8 fusion.21
  153.3 11.9 %collective-permute-done.14 = f32[384,768]{1,0:T(8,128)} collective-permute-done((f32[384,768]{1,0:T(8,128)}, f32[384,768]{1,0:T(8,128)}, u32[]{:S(2)}, u32[]{:S(2)}) %collective-permute-start.14) | collective-permute-done | bytes 1179680 | tf_op jit(solution)/shard_map/A10/ppermute | solution.py:218
  165.2 2.4 dynamic-slice_add_fusion.6
  172.8 22.8 %B0.1 = (bf16[256,768]{1,0:T(8,128)(2,1)S(1)}, f32[256,768]{1,0:T(8,128)S(1)}, f32[8,768]{1,0:T(8,128)S(1)}, f32[64,768]{1,0:T(8,128)S(1)}, f32[64,768]{1,0:T(8,128)S(1)}, /*index=5*/f32[8,768]{1,0:T(8,128)S(1)}) custom-call(f32[256,768]{1,0:T(8,128)S(1)} %copy-done.20, f32[256,768]{1,0:T(8,128)S(1)} %copy-done.8, f32[256,768]{1,0:T(8,128)S(1)} %copy-done.18, ...), custom_call_target="tpu_custom_call" | custom-call | bytes 78200000 | tf_op jit(solution)/shard_map/B0/pallas_call | solution.py:23
  195.7 2.7 dynamic-slice_add_fusion.8
  202.8 5.3 %collective-permute-start.23 = (f32[96,768]{1,0:T(8,128)S(1)}, f32[96,768]{1,0:T(8,128)S(1)}, u32[]{:S(2)}, u32[]{:S(2)}) collective-permute-start(f32[96,768]{1,0:T(8,128)S(1)} %dynamic-slice_add_fusion.15), channel_id=1, source_target_pairs={{0,8},{1,9},{2,10},{3,11},{4,12},{5,13},{6,14},{7,15},{8,0},{9,1},... | collective-permute-start | bytes 884744 | tf_op jit(solution)/shard_map/A30/ppermute | solution.py:218
  208.1 4.1 dynamic-slice_add_fusion
  213.9 1.9 dynamic-slice_add_fusion.13
  217.5 1.9 add_add_fusion.4
  226.3 2.1 R.1
  228.7 2.9 dynamic-slice_add_fusion.4
  236.1 13.4 %collective-permute-done.25 = f32[96,768]{1,0:T(8,128)} collective-permute-done((f32[96,768]{1,0:T(8,128)S(1)}, f32[96,768]{1,0:T(8,128)}, u32[]{:S(2)}, u32[]{:S(2)}) %collective-permute-start.25) | collective-permute-done | bytes 294944 | tf_op jit(solution)/shard_map/A40/ppermute | solution.py:218
  253.0 21.7 %collective-permute-done.29 = f32[48,768]{1,0:T(8,128)S(1)} collective-permute-done((f32[48,768]{1,0:T(8,128)S(1)}, f32[48,768]{1,0:T(8,128)S(1)}, u32[]{:S(2)}, u32[]{:S(2)}) %collective-permute-start.29) | collective-permute-done | bytes 147488 | tf_op jit(solution)/shard_map/A32/ppermute | solution.py:218
  274.7 3.4 collective-permute-start.30
  278.2 2.6 fusion.16
  282.5 2.8 collective-permute-done.30
  288.1 2.7 collective-permute-start.33
  294.8 5.0 %collective-permute-done.34 = f32[48,1536]{1,0:T(8,128)} collective-permute-done((f32[48,1536]{1,0:T(8,128)S(1)}, f32[48,1536]{1,0:T(8,128)}, u32[]{:S(2)}, u32[]{:S(2)}) %collective-permute-start.34) | collective-permute-done | bytes 294944 | tf_op jit(solution)/shard_map/A31/ppermute | solution.py:218
  301.0 5.3 %collective-permute-done.33 = f32[96,768]{1,0:T(8,128)S(1)} collective-permute-done((f32[96,768]{1,0:T(8,128)}, f32[96,768]{1,0:T(8,128)S(1)}, u32[]{:S(2)}, u32[]{:S(2)}) %collective-permute-start.33) | collective-permute-done | bytes 294944 | tf_op jit(solution)/shard_map/A52/ppermute | solution.py:218
  310.3 3.9 collective-permute-done.38
  317.3 9.1 %collective-permute-done.43 = f32[96,1536]{1,0:T(8,128)S(1)} collective-permute-done((f32[96,1536]{1,0:T(8,128)S(1)}, f32[96,1536]{1,0:T(8,128)S(1)}, u32[]{:S(2)}, u32[]{:S(2)}) %collective-permute-start.43) | collective-permute-done | bytes 589856 | tf_op jit(solution)/shard_map/A51/ppermute | solution.py:218
  329.1 2.9 collective-permute-start.40
  332.0 26.4 %collective-permute-done.41.refs_1_ = f32[768,768]{1,0:T(8,128)} collective-permute-done((f32[768,768]{1,0:T(8,128)}, f32[768,768]{1,0:T(8,128)}, u32[]{:S(2)}, u32[]{:S(2)}) %collective-permute-start.41) | collective-permute-done | bytes 2359328 | tf_op jit(solution)/shard_map/A70/ppermute | solution.py:218
  359.9 9.7 %collective-permute-done.46 = f32[56,768]{1,0:T(8,128)S(1)} collective-permute-done((f32[56,768]{1,0:T(8,128)S(1)}, f32[56,768]{1,0:T(8,128)S(1)}, u32[]{:S(2)}, u32[]{:S(2)}) %collective-permute-start.46) | collective-permute-done | bytes 172064 | tf_op jit(solution)/shard_map/A43/ppermute | solution.py:218
  373.7 2.4 collective-permute-done.44.refs_1_
  376.1 8.3 %J0.1 = f32[3072,768]{1,0:T(8,128)} custom-call(s32[5]{0:T(128)S(1)} %stack.17.places_ref, f32[768,768]{1,0:T(8,128)} %pad_maximum_fusion.1.refs_0_, f32[768,768]{1,0:T(8,128)} %collective-permute-done.41.refs_1_, f32[768,768]{1,0:T(8,128)} %collective-permute-done.51.refs_2_, f32[768,768]{1,0:T(8,128)} %collective-permute-done.52.refs_3_), custom_call_target="tpu_custom_call" | custom-call | bytes 18874368 | tf_op jit(solution)/shard_map/J0/pallas_call | solution.py:281
  387.1 16.9 %collective-permute-done.53 = f32[224,768]{1,0:T(8,128)S(1)} collective-permute-done((f32[224,768]{1,0:T(8,128)S(1)}, f32[224,768]{1,0:T(8,128)S(1)}, u32[]{:S(2)}, u32[]{:S(2)}) %collective-permute-start.53) | collective-permute-done | bytes 688160 | tf_op jit(solution)/shard_map/A63/ppermute | solution.py:218
  404.2 5.9 %collective-permute-done.49.refs_1_ = f32[384,1536]{1,0:T(8,128)} collective-permute-done((f32[384,1536]{1,0:T(8,128)}, f32[384,1536]{1,0:T(8,128)}, u32[]{:S(2)}, u32[]{:S(2)}) %collective-permute-start.49) | collective-permute-done | bytes 2359328 | tf_op jit(solution)/shard_map/A71/ppermute | solution.py:218
  411.1 6.9 %collective-permute-done.48.refs_3_ = f32[384,768]{1,0:T(8,128)S(1)} collective-permute-done((f32[384,768]{1,0:T(8,128)S(1)}, f32[384,768]{1,0:T(8,128)S(1)}, u32[]{:S(2)}, u32[]{:S(2)}) %collective-permute-start.48) | collective-permute-done | bytes 1179680 | tf_op jit(solution)/shard_map/F2/ppermute | solution.py:221
  418.0 3.4 collective-permute-done.47.refs_2_
  421.4 3.8 J2.1
  425.2 6.8 %J1.1 = f32[768,3072]{1,0:T(8,128)} custom-call(s32[5]{0:T(128)S(1)} %stack.17.places_ref, f32[384,1536]{1,0:T(8,128)} %pad_maximum_fusion.2.refs_0_, f32[384,1536]{1,0:T(8,128)} %collective-permute-done.49.refs_1_, f32[384,1536]{1,0:T(8,128)S(1)} %collective-permute-done.55.refs_2_, f32[384,1536]{1,0:T(8,128)S(1)} %collective-permute-done.56.refs_3_), custom_call_target="tpu_custom_call" | custom-call | bytes 18874368 | tf_op jit(solution)/shard_map/J1/pallas_call | solution.py:281
  432.6 2.1 fusion.8
  435.2 2.0 collective-permute-done.57.refs_2_
  437.2 3.5 J3.1
  (406 shorter events, 106.5 us)
Async XLA Ops:
  3.2 8.3 %collective-permute-start = (f32[8,768]{1,0:T(8,128)S(1)}, f32[8,768]{1,0:T(8,128)S(1)}, u32[]{:S(2)}, u32[]{:S(2)}) collective-permute-start(f32[8,768]{1,0:T(8,128)S(1)} %fusion.50), channel_id=1, source_target_pairs={{0,1},{1,2},{2,3},{3,4},{4,5},{5,6},{6,7},{7,8},{8,9},{9,10},{10,1... | collective-permute-start | bytes 73736 | tf_op jit(solution)/shard_map/ppermute | solution.py:497
  18.0 6.5 %collective-permute-start.1 = (f32[64,768]{1,0:T(8,128)S(1)}, f32[64,768]{1,0:T(8,128)}, u32[]{:S(2)}, u32[]{:S(2)}) collective-permute-start(f32[64,768]{1,0:T(8,128)S(1)} %get-tuple-element.83), channel_id=1, source_target_pairs={{0,1},{1,0},{2,3},{3,2},{4,5},{5,4},{6,7},{7,6},{8,9},{9,8},{10,11... | collective-permute-start | bytes 589832 | tf_op jit(solution)/shard_map/ppermute | solution.py:420
  26.3 5.9 %collective-permute-start.2 = (f32[64,768]{1,0:T(8,128)}, f32[64,768]{1,0:T(8,128)S(1)}, u32[]{:S(2)}, u32[]{:S(2)}) collective-permute-start(f32[64,768]{1,0:T(8,128)} %get-tuple-element.222), channel_id=1, source_target_pairs={{0,2},{1,3},{2,0},{3,1},{4,6},{5,7},{6,4},{7,5},{8,10},{9,11},{10,... | collective-permute-start | bytes 589832 | tf_op jit(solution)/shard_map/ppermute | solution.py:420
  33.9 5.9 %collective-permute-start.3 = (f32[64,768]{1,0:T(8,128)}, f32[64,768]{1,0:T(8,128)S(1)}, u32[]{:S(2)}, u32[]{:S(2)}) collective-permute-start(f32[64,768]{1,0:T(8,128)} %select_add_fusion.4), channel_id=1, source_target_pairs={{0,4},{1,5},{2,6},{3,7},{4,0},{5,1},{6,2},{7,3},{8,12},{9,13},{10,... | collective-permute-start | bytes 589832 | tf_op jit(solution)/shard_map/ppermute | solution.py:420
  40.7 8.7 %collective-permute-start.4 = (f32[64,768]{1,0:T(8,128)S(1)}, f32[64,768]{1,0:T(8,128)S(1)}, u32[]{:S(2)}, u32[]{:S(2)}) collective-permute-start(f32[64,768]{1,0:T(8,128)S(1)} %select_add_fusion.3), channel_id=1, source_target_pairs={{0,8},{1,9},{2,10},{3,11},{4,12},{5,13},{6,14},{7,15},{8,0},{9,1},... | collective-permute-start | bytes 589832 | tf_op jit(solution)/shard_map/ppermute | solution.py:420
  67.9 8.4 %collective-permute-start.5 = (f32[256,1536]{1,0:T(8,128)}, f32[256,1536]{1,0:T(8,128)}, u32[]{:S(2)}, u32[]{:S(2)}) collective-permute-start(f32[256,1536]{1,0:T(8,128)} %get-tuple-element.183), channel_id=1, source_target_pairs={{0,16},{16,0},{1,17},{17,1},{2,18},{18,2},{3,19},{19,3},{4,20},{20... | collective-permute-start | bytes 4718600 | tf_op jit(solution)/shard_map/X/ppermute | solution.py:221
  68.9 3.9 collective-permute-start.6
  69.4 36.0 %collective-permute-start.16 = (f32[256,768]{1,0:T(8,128)}, f32[256,768]{1,0:T(8,128)}, u32[]{:S(2)}, u32[]{:S(2)}) collective-permute-start(f32[256,768]{1,0:T(8,128)} %get-tuple-element.159), channel_id=1, source_target_pairs={{0,16},{16,0},{1,17},{17,1},{2,18},{18,2},{3,19},{19,3},{4,20},{20... | collective-permute-start | bytes 2359304 | tf_op jit(solution)/shard_map/ppermute | solution.py:221
  75.8 47.9 %collective-permute-start.11 = (f32[256,768]{1,0:T(8,128)}, f32[256,768]{1,0:T(8,128)}, u32[]{:S(2)}, u32[]{:S(2)}) collective-permute-start(f32[256,768]{1,0:T(8,128)} %get-tuple-element.161), channel_id=1, source_target_pairs={{0,16},{16,0},{1,17},{17,1},{2,18},{18,2},{3,19},{19,3},{4,20},{20... | collective-permute-start | bytes 2359304 | tf_op jit(solution)/shard_map/X/ppermute | solution.py:221
  76.0 29.9 %collective-permute-start.15 = (f32[256,768]{1,0:T(8,128)}, f32[256,768]{1,0:T(8,128)}, u32[]{:S(2)}, u32[]{:S(2)}) collective-permute-start(f32[256,768]{1,0:T(8,128)} %convert_element_type.91), channel_id=1, source_target_pairs={{0,16},{16,0},{1,17},{17,1},{2,18},{18,2},{3,19},{19,3},{4,20},{20... | collective-permute-start | bytes 2359304 | tf_op jit(solution)/shard_map/K1/ppermute | solution.py:221
  86.1 45.6 %collective-permute-start.9 = (f32[768,768]{1,0:T(8,128)}, f32[768,768]{1,0:T(8,128)}, u32[]{:S(2)}, u32[]{:S(2)}) collective-permute-start(f32[768,768]{1,0:T(8,128)} %fusion.11), channel_id=1, source_target_pairs={{0,1},{1,0},{2,3},{3,2},{4,5},{5,4},{6,7},{7,6},{8,9},{9,8},{10,11... | collective-permute-start | bytes 7077896 | tf_op jit(solution)/shard_map/A00/ppermute | solution.py:218
  96.7 31.3 %collective-permute-start.12 = (f32[256,1536]{1,0:T(8,128)}, f32[256,1536]{1,0:T(8,128)}, u32[]{:S(2)}, u32[]{:S(2)}) collective-permute-start(f32[256,1536]{1,0:T(8,128)} %get-tuple-element.181), channel_id=1, source_target_pairs={{0,16},{16,0},{1,17},{17,1},{2,18},{18,2},{3,19},{19,3},{4,20},{20... | collective-permute-start | bytes 4718600 | tf_op jit(solution)/shard_map/G1/ppermute | solution.py:221
  105.4 20.5 %collective-permute-start.17 = (f32[256,768]{1,0:T(8,128)}, f32[256,768]{1,0:T(8,128)}, u32[]{:S(2)}, u32[]{:S(2)}) collective-permute-start(f32[256,768]{1,0:T(8,128)} %get-tuple-element.204), channel_id=1, source_target_pairs={{0,16},{16,0},{1,17},{17,1},{2,18},{18,2},{3,19},{19,3},{4,20},{20... | collective-permute-start | bytes 2359304 | tf_op jit(solution)/shard_map/K1/ppermute | solution.py:221
  105.9 13.5 %collective-permute-start.7 = (f32[64,768]{1,0:T(8,128)S(1)}, f32[64,768]{1,0:T(8,128)S(1)}, u32[]{:S(2)}, u32[]{:S(2)}) collective-permute-start(f32[64,768]{1,0:T(8,128)S(1)} %get-tuple-element.90), channel_id=1, source_target_pairs={{0,1},{1,0},{2,3},{3,2},{4,5},{5,4},{6,7},{7,6},{8,9},{9,8},{10,11... | collective-permute-start | bytes 589832 | tf_op jit(solution)/shard_map/K1/ppermute | solution.py:420
  120.1 16.3 %collective-permute-start.8 = (f32[64,768]{1,0:T(8,128)}, f32[64,768]{1,0:T(8,128)S(1)}, u32[]{:S(2)}, u32[]{:S(2)}) collective-permute-start(f32[64,768]{1,0:T(8,128)} %select_add_fusion.2), channel_id=1, source_target_pairs={{0,2},{1,3},{2,0},{3,1},{4,6},{5,7},{6,4},{7,5},{8,10},{9,11},{10,... | collective-permute-start | bytes 589832 | tf_op jit(solution)/shard_map/P/ppermute | solution.py:420
  136.0 29.2 %collective-permute-start.14 = (f32[384,768]{1,0:T(8,128)}, f32[384,768]{1,0:T(8,128)}, u32[]{:S(2)}, u32[]{:S(2)}) collective-permute-start(f32[384,768]{1,0:T(8,128)} %get-tuple-element.168), channel_id=1, source_target_pairs={{0,2},{1,3},{2,0},{3,1},{4,6},{5,7},{6,4},{7,5},{8,10},{9,11},{10,... | collective-permute-start | bytes 3538952 | tf_op jit(solution)/shard_map/A10/ppermute | solution.py:218
  137.5 6.7 %collective-permute-start.10 = (f32[64,768]{1,0:T(8,128)S(1)}, f32[64,768]{1,0:T(8,128)S(1)}, u32[]{:S(2)}, u32[]{:S(2)}) collective-permute-start(f32[64,768]{1,0:T(8,128)S(1)} %select_add_fusion.1), channel_id=1, source_target_pairs={{0,4},{1,5},{2,6},{3,7},{4,0},{5,1},{6,2},{7,3},{8,12},{9,13},{10,... | collective-permute-start | bytes 589832 | tf_op jit(solution)/shard_map/P/ppermute | solution.py:420
  140.6 67.5 %collective-permute-start.21 = (f32[384,1536]{1,0:T(8,128)}, f32[384,1536]{1,0:T(8,128)}, u32[]{:S(2)}, u32[]{:S(2)}) collective-permute-start(f32[384,1536]{1,0:T(8,128)} %fusion.27), channel_id=1, source_target_pairs={{0,1},{1,0},{2,3},{3,2},{4,5},{5,4},{6,7},{7,6},{8,9},{9,8},{10,11... | collective-permute-start | bytes 7077896 | tf_op jit(solution)/shard_map/A01/ppermute | solution.py:218
  146.5 49.2 %collective-permute-start.19 = (f32[384,768]{1,0:T(8,128)}, f32[384,768]{1,0:T(8,128)}, u32[]{:S(2)}, u32[]{:S(2)}) collective-permute-start(f32[384,768]{1,0:T(8,128)} %fusion.23), channel_id=1, source_target_pairs={{0,1},{1,0},{2,3},{3,2},{4,5},{5,4},{6,7},{7,6},{8,9},{9,8},{10,11... | collective-permute-start | bytes 3538952 | tf_op jit(solution)/shard_map/A02/ppermute | solution.py:218
  148.3 20.0 %collective-permute-start.13 = (f32[64,768]{1,0:T(8,128)}, f32[64,768]{1,0:T(8,128)}, u32[]{:S(2)}, u32[]{:S(2)}) collective-permute-start(f32[64,768]{1,0:T(8,128)} %select_add_fusion), channel_id=1, source_target_pairs={{0,8},{1,9},{2,10},{3,11},{4,12},{5,13},{6,14},{7,15},{8,0},{9,1},... | collective-permute-start | bytes 589832 | tf_op jit(solution)/shard_map/P/ppermute | solution.py:420
  167.6 34.2 %collective-permute-start.22 = (f32[192,768]{1,0:T(8,128)}, f32[192,768]{1,0:T(8,128)}, u32[]{:S(2)}, u32[]{:S(2)}) collective-permute-start(f32[192,768]{1,0:T(8,128)} %get-tuple-element.180), channel_id=1, source_target_pairs={{0,4},{1,5},{2,6},{3,7},{4,0},{5,1},{6,2},{7,3},{8,12},{9,13},{10,... | collective-permute-start | bytes 1769480 | tf_op jit(solution)/shard_map/A20/ppermute | solution.py:218
  172.8 22.9 %copy-start.53 = (f32[384,768]{1,0:T(8,128)S(1)}, f32[384,768]{1,0:T(8,128)}, u32[]{:S(2)}) copy-start(f32[384,768]{1,0:T(8,128)} %fusion.21) | copy-start | bytes 3538948
  198.5 15.4 %collective-permute-start.20 = (f32[192,768]{1,0:T(8,128)}, f32[192,768]{1,0:T(8,128)}, u32[]{:S(2)}, u32[]{:S(2)}) collective-permute-start(f32[192,768]{1,0:T(8,128)} %get-tuple-element.178), channel_id=1, source_target_pairs={{0,2},{1,3},{2,0},{3,1},{4,6},{5,7},{6,4},{7,5},{8,10},{9,11},{10,... | collective-permute-start | bytes 1769480 | tf_op jit(solution)/shard_map/A12/ppermute | solution.py:218
  199.3 16.5 %collective-permute-start.18 = (f32[8,768]{1,0:T(8,128)}, f32[8,768]{1,0:T(8,128)S(1)}, u32[]{:S(2)}, u32[]{:S(2)}) collective-permute-start(f32[8,768]{1,0:T(8,128)} %copy-done.29), channel_id=1, source_target_pairs={{1,0},{2,1},{3,2},{4,3},{5,4},{6,5},{7,6},{8,7},{9,8},{10,9},{11,1... | collective-permute-start | bytes 73736 | tf_op jit(solution)/shard_map/B0/ppermute | solution.py:596
  202.8 14.7 %collective-permute-start.23 = (f32[96,768]{1,0:T(8,128)S(1)}, f32[96,768]{1,0:T(8,128)S(1)}, u32[]{:S(2)}, u32[]{:S(2)}) collective-permute-start(f32[96,768]{1,0:T(8,128)S(1)} %dynamic-slice_add_fusion.15), channel_id=1, source_target_pairs={{0,8},{1,9},{2,10},{3,11},{4,12},{5,13},{6,14},{7,15},{8,0},{9,1},... | collective-permute-start | bytes 884744 | tf_op jit(solution)/shard_map/A30/ppermute | solution.py:218
  212.2 16.5 %collective-permute-start.26 = (f32[192,1536]{1,0:T(8,128)}, f32[192,1536]{1,0:T(8,128)}, u32[]{:S(2)}, u32[]{:S(2)}) collective-permute-start(f32[192,1536]{1,0:T(8,128)} %get-tuple-element.166), channel_id=1, source_target_pairs={{0,2},{1,3},{2,0},{3,1},{4,6},{5,7},{6,4},{7,5},{8,10},{9,11},{10,... | collective-permute-start | bytes 3538952 | tf_op jit(solution)/shard_map/A11/ppermute | solution.py:218
  222.5 3.0 collective-permute-start.27
  222.7 2.7 collective-permute-start.28
  233.3 44.9 %collective-permute-start.32 = (f32[448,768]{1,0:T(8,128)}, f32[448,768]{1,0:T(8,128)}, u32[]{:S(2)}, u32[]{:S(2)}) collective-permute-start(f32[448,768]{1,0:T(8,128)} %pad_maximum_fusion.3), channel_id=1, source_target_pairs={{0,1},{1,0},{2,3},{3,2},{4,5},{5,4},{6,7},{7,6},{8,9},{9,8},{10,11... | collective-permute-start | bytes 4128776 | tf_op jit(solution)/shard_map/A03/ppermute | solution.py:218
  234.1 15.4 %collective-permute-start.25 = (f32[96,768]{1,0:T(8,128)S(1)}, f32[96,768]{1,0:T(8,128)}, u32[]{:S(2)}, u32[]{:S(2)}) collective-permute-start(f32[96,768]{1,0:T(8,128)S(1)} %copy-done.72), channel_id=1, source_target_pairs={{0,8},{1,9},{2,10},{3,11},{4,12},{5,13},{6,14},{7,15},{8,0},{9,1},... | collective-permute-start | bytes 884744 | tf_op jit(solution)/shard_map/A40/ppermute | solution.py:218
  234.1 16.5 %collective-permute-start.24 = (f32[96,768]{1,0:T(8,128)}, f32[96,768]{1,0:T(8,128)S(1)}, u32[]{:S(2)}, u32[]{:S(2)}) collective-permute-start(f32[96,768]{1,0:T(8,128)} %get-tuple-element.199), channel_id=1, source_target_pairs={{0,4},{1,5},{2,6},{3,7},{4,0},{5,1},{6,2},{7,3},{8,12},{9,13},{10,... | collective-permute-start | bytes 884744 | tf_op jit(solution)/shard_map/A22/ppermute | solution.py:218
  235.9 46.5 %collective-permute-start.31 = (f32[96,1536]{1,0:T(8,128)}, f32[96,1536]{1,0:T(8,128)S(1)}, u32[]{:S(2)}, u32[]{:S(2)}) collective-permute-start(f32[96,1536]{1,0:T(8,128)} %get-tuple-element.176), channel_id=1, source_target_pairs={{0,4},{1,5},{2,6},{3,7},{4,0},{5,1},{6,2},{7,3},{8,12},{9,13},{10,... | collective-permute-start | bytes 1769480 | tf_op jit(solution)/shard_map/A21/ppermute | solution.py:218
  250.6 35.5 %collective-permute-start.36 = (f32[192,768]{1,0:T(8,128)S(1)}, f32[192,768]{1,0:T(8,128)S(1)}, u32[]{:S(2)}, u32[]{:S(2)}) collective-permute-start(f32[192,768]{1,0:T(8,128)S(1)} %pad_maximum_fusion.9), channel_id=1, source_target_pairs={{0,4},{1,5},{2,6},{3,7},{4,0},{5,1},{6,2},{7,3},{8,12},{9,13},{10,... | collective-permute-start | bytes 1769480 | tf_op jit(solution)/shard_map/A50/ppermute | solution.py:218
  250.7 24.0 %collective-permute-start.29 = (f32[48,768]{1,0:T(8,128)S(1)}, f32[48,768]{1,0:T(8,128)S(1)}, u32[]{:S(2)}, u32[]{:S(2)}) collective-permute-start(f32[48,768]{1,0:T(8,128)S(1)} %dynamic-slice_add_fusion.19), channel_id=1, source_target_pairs={{0,8},{1,9},{2,10},{3,11},{4,12},{5,13},{6,14},{7,15},{8,0},{9,1},... | collective-permute-start | bytes 442376 | tf_op jit(solution)/shard_map/A32/ppermute | solution.py:218
  274.7 10.5 %collective-permute-start.30 = (f32[48,768]{1,0:T(8,128)S(1)}, f32[48,768]{1,0:T(8,128)S(1)}, u32[]{:S(2)}, u32[]{:S(2)}) collective-permute-start(f32[48,768]{1,0:T(8,128)S(1)} %add_add_fusion.6), channel_id=1, source_target_pairs={{0,8},{1,9},{2,10},{3,11},{4,12},{5,13},{6,14},{7,15},{8,0},{9,1},... | collective-permute-start | bytes 442376 | tf_op jit(solution)/shard_map/A42/ppermute | solution.py:218
  280.7 11.3 %collective-permute-start.35 = (f32[224,768]{1,0:T(8,128)}, f32[224,768]{1,0:T(8,128)}, u32[]{:S(2)}, u32[]{:S(2)}) collective-permute-start(f32[224,768]{1,0:T(8,128)} %get-tuple-element.170), channel_id=1, source_target_pairs={{0,2},{1,3},{2,0},{3,1},{4,6},{5,7},{6,4},{7,5},{8,10},{9,11},{10,... | collective-permute-start | bytes 2064392 | tf_op jit(solution)/shard_map/A13/ppermute | solution.py:218
  287.3 20.0 %collective-permute-start.39 = (f32[384,768]{1,0:T(8,128)}, f32[384,768]{1,0:T(8,128)}, u32[]{:S(2)}, u32[]{:S(2)}) collective-permute-start(f32[384,768]{1,0:T(8,128)} %pad_maximum_fusion.5), channel_id=1, source_target_pairs={{0,2},{1,3},{2,0},{3,1},{4,6},{5,7},{6,4},{7,5},{8,10},{9,11},{10,... | collective-permute-start | bytes 3538952 | tf_op jit(solution)/shard_map/A60/ppermute | solution.py:218
  288.1 11.7 %collective-permute-start.34 = (f32[48,1536]{1,0:T(8,128)S(1)}, f32[48,1536]{1,0:T(8,128)}, u32[]{:S(2)}, u32[]{:S(2)}) collective-permute-start(f32[48,1536]{1,0:T(8,128)S(1)} %dynamic-slice_add_fusion.12), channel_id=1, source_target_pairs={{0,8},{1,9},{2,10},{3,11},{4,12},{5,13},{6,14},{7,15},{8,0},{9,1},... | collective-permute-start | bytes 884744 | tf_op jit(solution)/shard_map/A31/ppermute | solution.py:218
  288.1 18.2 %collective-permute-start.33 = (f32[96,768]{1,0:T(8,128)}, f32[96,768]{1,0:T(8,128)S(1)}, u32[]{:S(2)}, u32[]{:S(2)}) collective-permute-start(f32[96,768]{1,0:T(8,128)} %pad_maximum_fusion.14), channel_id=1, source_target_pairs={{0,4},{1,5},{2,6},{3,7},{4,0},{5,1},{6,2},{7,3},{8,12},{9,13},{10,... | collective-permute-start | bytes 884744 | tf_op jit(solution)/shard_map/A52/ppermute | solution.py:218
  293.2 20.9 %collective-permute-start.38 = (f32[112,768]{1,0:T(8,128)S(1)}, f32[112,768]{1,0:T(8,128)S(1)}, u32[]{:S(2)}, u32[]{:S(2)}) collective-permute-start(f32[112,768]{1,0:T(8,128)S(1)} %get-tuple-element.188), channel_id=1, source_target_pairs={{0,4},{1,5},{2,6},{3,7},{4,0},{5,1},{6,2},{7,3},{8,12},{9,13},{10,... | collective-permute-start | bytes 1032200 | tf_op jit(solution)/shard_map/A23/ppermute | solution.py:218
  300.9 13.3 %collective-permute-start.42 = (f32[48,1536]{1,0:T(8,128)S(1)}, f32[48,1536]{1,0:T(8,128)S(1)}, u32[]{:S(2)}, u32[]{:S(2)}) collective-permute-start(f32[48,1536]{1,0:T(8,128)S(1)} %add_add_fusion.3), channel_id=1, source_target_pairs={{0,8},{1,9},{2,10},{3,11},{4,12},{5,13},{6,14},{7,15},{8,0},{9,1},... | collective-permute-start | bytes 884744 | tf_op jit(solution)/shard_map/A41/ppermute | solution.py:218
  310.3 48.1 %collective-permute-start.41 = (f32[768,768]{1,0:T(8,128)}, f32[768,768]{1,0:T(8,128)}, u32[]{:S(2)}, u32[]{:S(2)}) collective-permute-start(f32[768,768]{1,0:T(8,128)} %pad_maximum_fusion.1.refs_0_), channel_id=1, source_target_pairs={{0,1},{1,0},{2,3},{3,2},{4,5},{5,4},{6,7},{7,6},{8,9},{9,8},{10,11... | collective-permute-start | bytes 7077896 | tf_op jit(solution)/shard_map/A70/ppermute | solution.py:218
  314.3 12.1 %collective-permute-start.43 = (f32[96,1536]{1,0:T(8,128)S(1)}, f32[96,1536]{1,0:T(8,128)S(1)}, u32[]{:S(2)}, u32[]{:S(2)}) collective-permute-start(f32[96,1536]{1,0:T(8,128)S(1)} %pad_maximum_fusion.11), channel_id=1, source_target_pairs={{0,4},{1,5},{2,6},{3,7},{4,0},{5,1},{6,2},{7,3},{8,12},{9,13},{10,... | collective-permute-start | bytes 1769480 | tf_op jit(solution)/shard_map/A51/ppermute | solution.py:218
  315.7 42.8 %collective-permute-start.37 = (f32[192,768]{1,0:T(8,128)}, f32[192,768]{1,0:T(8,128)}, u32[]{:S(2)}, u32[]{:S(2)}) collective-permute-start(f32[192,768]{1,0:T(8,128)} %pad_maximum_fusion.10), channel_id=1, source_target_pairs={{0,2},{1,3},{2,0},{3,1},{4,6},{5,7},{6,4},{7,5},{8,10},{9,11},{10,... | collective-permute-start | bytes 1769480 | tf_op jit(solution)/shard_map/A62/ppermute | solution.py:218
  326.5 33.2 %copy-start.48 = (f32[96,1536]{1,0:T(8,128)}, f32[96,1536]{1,0:T(8,128)S(1)}, u32[]{:S(2)}) copy-start(f32[96,1536]{1,0:T(8,128)S(1)} %get-tuple-element.195) | copy-start | bytes 1769476
  326.5 31.9 %copy-start.68 = (f32[112,768]{1,0:T(8,128)S(1)}, f32[112,768]{1,0:T(8,128)}, u32[]{:S(2)}) copy-start(f32[112,768]{1,0:T(8,128)} %copy-done.67) | copy-start | bytes 1032196
  326.5 32.0 %copy-start.60 = (f32[96,768]{1,0:T(8,128)S(1)}, f32[96,768]{1,0:T(8,128)}, u32[]{:S(2)}) copy-start(f32[96,768]{1,0:T(8,128)} %copy-done.59) | copy-start | bytes 884740
  326.5 31.9 %copy-start.83 = (f32[112,768]{1,0:T(8,128)S(1)}, f32[112,768]{1,0:T(8,128)}, u32[]{:S(2)}) copy-start(f32[112,768]{1,0:T(8,128)} %copy-done.82) | copy-start | bytes 1032196
  327.6 42.7 %collective-permute-start.45 = (f32[192,1536]{1,0:T(8,128)}, f32[192,1536]{1,0:T(8,128)}, u32[]{:S(2)}, u32[]{:S(2)}) collective-permute-start(f32[192,1536]{1,0:T(8,128)} %pad_maximum_fusion.6), channel_id=1, source_target_pairs={{0,2},{1,3},{2,0},{3,1},{4,6},{5,7},{6,4},{7,5},{8,10},{9,11},{10,... | collective-permute-start | bytes 3538952 | tf_op jit(solution)/shard_map/A61/ppermute | solution.py:218
  329.1 29.3 %collective-permute-start.40 = (f32[56,768]{1,0:T(8,128)S(1)}, f32[56,768]{1,0:T(8,128)S(1)}, u32[]{:S(2)}, u32[]{:S(2)}) collective-permute-start(f32[56,768]{1,0:T(8,128)S(1)} %dynamic-slice_add_fusion.18), channel_id=1, source_target_pairs={{0,8},{1,9},{2,10},{3,11},{4,12},{5,13},{6,14},{7,15},{8,0},{9,1},... | collective-permute-start | bytes 516104 | tf_op jit(solution)/shard_map/A33/ppermute | solution.py:218
  332.0 44.1 %collective-permute-start.51 = (f32[768,768]{1,0:T(8,128)}, f32[768,768]{1,0:T(8,128)}, u32[]{:S(2)}, u32[]{:S(2)}) collective-permute-start(f32[768,768]{1,0:T(8,128)} %pad_maximum_fusion.1.refs_0_), channel_id=1, source_target_pairs={{0,16},{16,0},{1,17},{17,1},{2,18},{18,2},{3,19},{19,3},{4,20},{20... | collective-permute-start | bytes 7077896 | tf_op jit(solution)/shard_map/A70/ppermute | solution.py:221
  358.4 17.7 %collective-permute-start.52 = (f32[768,768]{1,0:T(8,128)}, f32[768,768]{1,0:T(8,128)}, u32[]{:S(2)}, u32[]{:S(2)}) collective-permute-start(f32[768,768]{1,0:T(8,128)} %collective-permute-done.41.refs_1_), channel_id=1, source_target_pairs={{0,16},{16,0},{1,17},{17,1},{2,18},{18,2},{3,19},{19,3},{4,20},{20... | collective-permute-start | bytes 7077896 | tf_op jit(solution)/shard_map/F0/ppermute | solution.py:221
  358.5 11.1 %collective-permute-start.46 = (f32[56,768]{1,0:T(8,128)S(1)}, f32[56,768]{1,0:T(8,128)S(1)}, u32[]{:S(2)}, u32[]{:S(2)}) collective-permute-start(f32[56,768]{1,0:T(8,128)S(1)} %add_add_fusion.5), channel_id=1, source_target_pairs={{0,8},{1,9},{2,10},{3,11},{4,12},{5,13},{6,14},{7,15},{8,0},{9,1},... | collective-permute-start | bytes 516104 | tf_op jit(solution)/shard_map/A43/ppermute | solution.py:218
  359.8 16.3 %collective-permute-start.44 = (f32[384,768]{1,0:T(8,128)S(1)}, f32[384,768]{1,0:T(8,128)S(1)}, u32[]{:S(2)}, u32[]{:S(2)}) collective-permute-start(f32[384,768]{1,0:T(8,128)S(1)} %pad_maximum_fusion.7.refs_0_), channel_id=1, source_target_pairs={{0,1},{1,0},{2,3},{3,2},{4,5},{5,4},{6,7},{7,6},{8,9},{9,8},{10,11... | collective-permute-start | bytes 3538952 | tf_op jit(solution)/shard_map/A72/ppermute | solution.py:218
  373.6 36.5 %collective-permute-start.49 = (f32[384,1536]{1,0:T(8,128)}, f32[384,1536]{1,0:T(8,128)}, u32[]{:S(2)}, u32[]{:S(2)}) collective-permute-start(f32[384,1536]{1,0:T(8,128)} %pad_maximum_fusion.2.refs_0_), channel_id=1, source_target_pairs={{0,1},{1,0},{2,3},{3,2},{4,5},{5,4},{6,7},{7,6},{8,9},{9,8},{10,11... | collective-permute-start | bytes 7077896 | tf_op jit(solution)/shard_map/A71/ppermute | solution.py:218
  373.6 10.9 %collective-permute-start.50 = (f32[112,768]{1,0:T(8,128)}, f32[112,768]{1,0:T(8,128)}, u32[]{:S(2)}, u32[]{:S(2)}) collective-permute-start(f32[112,768]{1,0:T(8,128)} %pad_maximum_fusion.13), channel_id=1, source_target_pairs={{0,4},{1,5},{2,6},{3,7},{4,0},{5,1},{6,2},{7,3},{8,12},{9,13},{10,... | collective-permute-start | bytes 1032200 | tf_op jit(solution)/shard_map/A53/ppermute | solution.py:218
  385.5 18.4 %collective-permute-start.53 = (f32[224,768]{1,0:T(8,128)S(1)}, f32[224,768]{1,0:T(8,128)S(1)}, u32[]{:S(2)}, u32[]{:S(2)}) collective-permute-start(f32[224,768]{1,0:T(8,128)S(1)} %pad_maximum_fusion.8), channel_id=1, source_target_pairs={{0,2},{1,3},{2,0},{3,1},{4,6},{5,7},{6,4},{7,5},{8,10},{9,11},{10,... | collective-permute-start | bytes 2064392 | tf_op jit(solution)/shard_map/A63/ppermute | solution.py:218
  410.1 15.1 %collective-permute-start.56 = (f32[384,1536]{1,0:T(8,128)}, f32[384,1536]{1,0:T(8,128)S(1)}, u32[]{:S(2)}, u32[]{:S(2)}) collective-permute-start(f32[384,1536]{1,0:T(8,128)} %collective-permute-done.49.refs_1_), channel_id=1, source_target_pairs={{0,16},{16,0},{1,17},{17,1},{2,18},{18,2},{3,19},{19,3},{4,20},{20... | collective-permute-start | bytes 7077896 | tf_op jit(solution)/shard_map/F1/ppermute | solution.py:221
  410.1 15.1 %collective-permute-start.55 = (f32[384,1536]{1,0:T(8,128)}, f32[384,1536]{1,0:T(8,128)S(1)}, u32[]{:S(2)}, u32[]{:S(2)}) collective-permute-start(f32[384,1536]{1,0:T(8,128)} %pad_maximum_fusion.2.refs_0_), channel_id=1, source_target_pairs={{0,16},{16,0},{1,17},{17,1},{2,18},{18,2},{3,19},{19,3},{4,20},{20... | collective-permute-start | bytes 7077896 | tf_op jit(solution)/shard_map/A71/ppermute | solution.py:221
  410.6 21.4 %collective-permute-start.54 = (f32[448,768]{1,0:T(8,128)S(1)}, f32[448,768]{1,0:T(8,128)S(1)}, u32[]{:S(2)}, u32[]{:S(2)}) collective-permute-start(f32[448,768]{1,0:T(8,128)S(1)} %pad_maximum_fusion.4.refs_0_), channel_id=1, source_target_pairs={{0,1},{1,0},{2,3},{3,2},{4,5},{5,4},{6,7},{7,6},{8,9},{9,8},{10,11... | collective-permute-start | bytes 4128776 | tf_op jit(solution)/shard_map/A73/ppermute | solution.py:218
  410.6 7.4 %collective-permute-start.48 = (f32[384,768]{1,0:T(8,128)S(1)}, f32[384,768]{1,0:T(8,128)S(1)}, u32[]{:S(2)}, u32[]{:S(2)}) collective-permute-start(f32[384,768]{1,0:T(8,128)S(1)} %collective-permute-done.44.refs_1_), channel_id=1, source_target_pairs={{0,16},{16,0},{1,17},{17,1},{2,18},{18,2},{3,19},{19,3},{4,20},{20... | collective-permute-start | bytes 3538952 | tf_op jit(solution)/shard_map/F2/ppermute | solution.py:221
  410.6 10.8 %collective-permute-start.47 = (f32[384,768]{1,0:T(8,128)S(1)}, f32[384,768]{1,0:T(8,128)S(1)}, u32[]{:S(2)}, u32[]{:S(2)}) collective-permute-start(f32[384,768]{1,0:T(8,128)S(1)} %pad_maximum_fusion.7.refs_0_), channel_id=1, source_target_pairs={{0,16},{16,0},{1,17},{17,1},{2,18},{18,2},{3,19},{19,3},{4,20},{20... | collective-permute-start | bytes 3538952 | tf_op jit(solution)/shard_map/A72/ppermute | solution.py:221
  432.0 3.2 collective-permute-start.58
  432.2 5.0 %collective-permute-start.57 = (f32[448,768]{1,0:T(8,128)S(1)}, f32[448,768]{1,0:T(8,128)S(1)}, u32[]{:S(2)}, u32[]{:S(2)}) collective-permute-start(f32[448,768]{1,0:T(8,128)S(1)} %pad_maximum_fusion.4.refs_0_), channel_id=1, source_target_pairs={{0,16},{16,0},{1,17},{17,1},{2,18},{18,2},{3,19},{19,3},{4,20},{20... | collective-permute-start | bytes 4128776 | tf_op jit(solution)/shard_map/A73/ppermute | solution.py:221
  (104 other events, 474.0 us)
